TPU v7x, 32 devices: a whole 2x2x4 slice. The times are simulated.
32 devices in a mesh: tile: 4 (over x, core), bulk: 8 (over z, y).
Axes of the slice: x: 2, y: 2, z: 4, core: 2. Of those that a mesh axis runs over, the one named last changes fastest.
Arguments:
- coarse_now: float32 [256, 512, 128], P('tile', 'bulk'), may hold values from -6 to 6
- coarse_before: float32 [256, 512, 128], P('tile', 'bulk'), may hold values from -6 to 6
- coarse_courant: float32 [256, 512, 128], P('tile', 'bulk'), may hold values from 0.05 to 0.3
- coarse_absorb: float32 [256, 512, 128], P('tile', 'bulk'), may hold values from 0.02 to 0.3
- fine_now: float32 [64, 48, 2304], P(('tile', 'bulk')), may hold values from -6 to 6
- fine_before: float32 [64, 48, 2304], P(('tile', 'bulk')), may hold values from -6 to 6
- fine_courant: float32 [64, 48, 2304], P(('tile', 'bulk')), may hold values from 0.05 to 0.3
- fine_absorb: float32 [64, 48, 2304], P(('tile', 'bulk')), may hold values from 0.02 to 0.3
- box_anchor: int32 [64, 3], P(('tile', 'bulk')), may hold values from 0 to 496, as said below
- intersection: int32 [32, 4, 4], P(('tile', 'bulk')), may hold values from -1 to 112, as said below
Outputs:
- coarse_next: float32 [256, 512, 128], P('tile', 'bulk')
- coarse_last: float32 [256, 512, 128], P('tile', 'bulk')
- fine_next: float32 [64, 48, 2304], P(('tile', 'bulk'))
- fine_last: float32 [64, 48, 2304], P(('tile', 'bulk'))
Inputs may be any that keep to these rules, and one draw needn't show every extreme that they name: `box_anchor`: box b is held in the box order of the fine arrays, by device d = b // 2; its region of 16 coarse cells along each dimension from its anchor lies inside the coarse block of device d, d XOR 1, d XOR h or d XOR h XOR 1, where h is half the number of devices; anchors are multiples of 16, and no two regions share a cell. `intersection`: row 0 lists each box exactly once, in the block of the device whose coarse cells hold its region, -1 in unused entries; rows 1 to 3 give that region's first cell relative to the block (0 in unused entries), matching box_anchor. Some block holds exactly 4 boxes.
All inputs are finite; a program needn't handle non-finite values.
Results may differ from a plain program's by a relative error of at most 0.0001.
Values sent between devices are 32-bit elements; how exact they have to be, the bound alone decides.
A program may use at most 512 MiB of HBM per device.

v0:
```python
import jax
import jax.numpy as jnp
from jax import lax
from jax.sharding import PartitionSpec as P

STEPS = 2


exact = lax.Precision.HIGHEST


def extended(array, sides, width):
    for axis, dim in sides:
        size, length = (lax.axis_size(axis), array.shape[dim])
        up = [(i, (i + 1) % size) for i in range(size - 1)]
        down = [(j, i) for i, j in up]
        last = lax.slice_in_dim(array, length - width, length, axis=dim)
        first = lax.slice_in_dim(array, 0, width, axis=dim)
        before = lax.ppermute(last, axis, up)
        after = lax.ppermute(first, axis, down)
        array = jnp.concatenate([before, array, after], axis=dim)
    return array


def fine_update(field, before, courant, absorb, ghosts):
    xm = jnp.concatenate([ghosts[0][None], field[:-1]], 0)
    xp = jnp.concatenate([field[1:], ghosts[1][None]], 0)
    ym = jnp.concatenate([ghosts[2][:, None, :], field[:, :-1]], 1)
    yp = jnp.concatenate([field[:, 1:], ghosts[3][:, None, :]], 1)
    zm = jnp.concatenate([ghosts[4][:, :, None], field[:, :, :-1]], 2)
    zp = jnp.concatenate([field[:, :, 1:], ghosts[5][:, :, None]], 2)
    lap = xm + xp + ym + yp + zm + zp - 6.0 * field
    return (2.0 * field - (1.0 - absorb) * before + courant * lap) / (1.0 + absorb)


def upsample(faces):
    return jnp.repeat(jnp.repeat(faces, 3, axis=-2), 3, axis=-1)


def coarse_update(padded, now, before, courant, absorb):
    centre = padded[1:-1, 1:-1, 1:-1]
    beside = padded[2:, 1:-1, 1:-1] + padded[:-2, 1:-1, 1:-1]
    beside = beside + padded[1:-1, 2:, 1:-1] + padded[1:-1, :-2, 1:-1]
    beside = beside + padded[1:-1, 1:-1, 2:] + padded[1:-1, 1:-1, :-2]
    lap = beside - 6.0 * centre
    return (2.0 * now - (1.0 - absorb) * before + courant * lap) / (1.0 + absorb)


def box_faces(padded, start, edge):
    cube = lax.dynamic_slice(padded, (start[0], start[1], start[2]), (edge + 2, edge + 2, edge + 2))
    inner = slice(1, edge + 1)
    return jnp.stack(
        [
            cube[0, inner, inner],
            cube[edge + 1, inner, inner],
            cube[inner, 0, inner],
            cube[inner, edge + 1, inner],
            cube[inner, inner, 0],
            cube[inner, inner, edge + 1],
        ]
    )


def old_rim(field):
    grown = extended(field, (("tile", 0), ("bulk", 1)), 1)
    return jnp.pad(grown, ((0, 0), (0, 0), (1, 1)))


def new_rim(field):
    grown = extended(field, (("tile", 0), ("bulk", 1)), 1)
    return jnp.pad(grown, ((0, 0), (0, 0), (1, 1)))


def on_device(
    coarse_now,
    coarse_before,
    coarse_courant,
    coarse_absorb,
    fine_now,
    fine_before,
    fine_courant,
    fine_absorb,
    box_anchor,
    intersection,
):
    cells_x, cells_y, depth = coarse_now.shape
    boxes_here, side, plane = fine_now.shape
    edge = side // 3
    n_bulk = lax.axis_size("bulk")
    devices = lax.axis_size("tile") * n_bulk
    slots = devices * boxes_here
    idents = intersection[0, 0]
    valid = idents >= 0
    starts = intersection[0, 1:]
    most = idents.shape[0]
    picker = (idents[:, None] == jnp.arange(slots, dtype=jnp.int32)[None, :]).astype(jnp.float32)
    source = box_anchor[:, 0] // cells_x * n_bulk + box_anchor[:, 1] // cells_y
    chooser = (source[:, None] == jnp.arange(devices, dtype=jnp.int32)[None, :]).astype(jnp.float32)
    shape = (boxes_here, side, side, side)
    fine = fine_now.reshape(shape)
    fine_prev = fine_before.reshape(shape)
    fine_c = fine_courant.reshape(shape)
    fine_a = fine_absorb.reshape(shape)
    faces_all = jax.vmap(box_faces, (None, 0, None))
    now = coarse_now
    before = coarse_before
    for step in range(STEPS):
        padded = old_rim(now)
        new = coarse_update(padded, now, before, coarse_courant, coarse_absorb)
        padded_new = new_rim(new)
        stacked = jnp.stack(
            [faces_all(padded, starts.T, edge), faces_all(padded_new, starts.T, edge)], axis=1
        )
        payload = stacked.reshape(most, 12, edge * edge)
        outgoing = jnp.einsum("ks,kpq->spq", picker, payload, precision=exact).reshape(
            devices, boxes_here, 12, edge * edge
        )
        arrived = lax.all_to_all(
            outgoing, ("tile", "bulk"), split_axis=0, concat_axis=0, tiled=True
        )
        taken = jnp.einsum("jd,djpq->jpq", chooser, arrived, precision=exact)
        taken = taken.reshape(boxes_here, 2, 6, edge, edge)
        for sub in range(3):
            weight = sub / 3.0
            ghosts = upsample(taken[:, 0] + weight * (taken[:, 1] - taken[:, 0]))
            ahead = jax.vmap(fine_update)(fine, fine_prev, fine_c, fine_a, ghosts)
            fine_prev = fine
            fine = ahead
        restricted = (
            fine.reshape(boxes_here, edge, 3, edge, 3, edge, 3)
            .mean(axis=(2, 4, 6))
            .reshape(boxes_here, edge * edge * edge)
        )
        outgoing_back = jnp.einsum("jd,jr->djr", chooser, restricted, precision=exact)
        returned = lax.all_to_all(
            outgoing_back, ("tile", "bulk"), split_axis=0, concat_axis=0, tiled=True
        )
        blocks = jnp.einsum(
            "ks,sr->kr", picker, returned.reshape(slots, edge * edge * edge), precision=exact
        )
        blocks = blocks.reshape(most, edge, edge, edge)
        for entry in range(most):
            corner = (starts[0, entry], starts[1, entry], starts[2, entry])
            current = lax.dynamic_slice(new, corner, (edge, edge, edge))
            new = lax.dynamic_update_slice(
                new, jnp.where(valid[entry], blocks[entry], current), corner
            )
        before = now
        now = new
    flat = (boxes_here, side, plane)
    return (now, before, fine.reshape(flat), fine_prev.reshape(flat))


def solution(mesh):
    in_specs = (
        P("tile", "bulk", None),
        P("tile", "bulk", None),
        P("tile", "bulk", None),
        P("tile", "bulk", None),
        P(("tile", "bulk"), None, None),
        P(("tile", "bulk"), None, None),
        P(("tile", "bulk"), None, None),
        P(("tile", "bulk"), None, None),
        P(("tile", "bulk"), None),
        P(("tile", "bulk"), None, None),
    )
    out_specs = (
        P("tile", "bulk", None),
        P("tile", "bulk", None),
        P(("tile", "bulk"), None, None),
        P(("tile", "bulk"), None, None),
    )
    return jax.shard_map(
        on_device, mesh=mesh, in_specs=in_specs, out_specs=out_specs, check_vma=False
    )
```

profile of v0, /device:TPU:0, one launch (start us, length us, event | category | flops | bytes accessed | tf_op | source)
XLA Modules:
  0.0 1369.5 jit_solution(1473371449460623986)
XLA Ops:
  20.0 38.8 %add.565 = f32[2,16,3,16,3,16,3]{6,5,4,3,2,1,0:T(8,128)} reshape(f32[2,48,2304]{2,1,0:T(8,128)S(1)} %get-tuple-element.276) | data formatting | bytes 1769472 | tf_op jit(solution)/shard_map/vmap()/add | solution.py:33
  61.7 38.7 %sub.175 = f32[2,16,3,16,3,16,3]{6,5,4,3,2,1,0:T(8,128)} reshape(f32[2,48,2304]{2,1,0:T(8,128)S(1)} %get-tuple-element.275) | data formatting | bytes 1769472 | tf_op jit(solution)/shard_map/vmap()/sub | solution.py:33
  101.9 38.7 %reshape.313 = f32[2,16,3,16,3,16,3]{6,5,4,3,2,1,0:T(8,128)} reshape(f32[2,48,2304]{2,1,0:T(8,128)S(1)} %copy-done.31) | data formatting | bytes 1769472 | tf_op jit(solution)/shard_map/reshape | solution.py:100
  144.1 39.8 %reshape.314 = f32[2,16,3,16,3,16,3]{6,5,4,3,2,1,0:T(8,128)} reshape(f32[2,48,2304]{2,1,0:T(8,128)} %param.15) | data formatting | bytes 1769472 | tf_op jit(solution)/shard_map/reshape | solution.py:101
  186.8 38.7 %reshape.315 = f32[2,16,3,16,3,16,3]{6,5,4,3,2,1,0:T(8,128)} reshape(f32[2,48,2304]{2,1,0:T(8,128)S(1)} %copy-done.29) | data formatting | bytes 1769472 | tf_op jit(solution)/shard_map/reshape | solution.py:102
  230.6 15.1 %while.4 = (s32[]{:T(128)}, f32[66,66,130]{2,1,0:T(8,128)}, s32[4,3]{1,0:T(4,128)S(1)}, f32[4,18,18,18]{3,2,1,0:T(8,128)S(1)}, s32[]{:T(128)}) while((s32[]{:T(128)}, f32[66,66,130]{2,1,0:T(8,128)}, s32[4,3]{1,0:T(4,128)S(1)}, f32[4,18,18,18]{3,2,1,0:T(8,128)S(1)}, s32[]{:T(128)}) %tuple.212), condition=%wide.while_cond, body=%wide.while_body.sunk | while | flops 2 | bytes 244649 | solution.py:50
  315.2 32.9 %copy.518 = f32[2,16,3,16,3,16,3]{5,3,6,4,2,1,0:T(8,128)} copy(f32[2,16,3,16,3,16,3]{6,5,4,3,2,1,0:T(8,128)} %add.565) | data formatting | bytes 1769472 | tf_op jit(solution)/shard_map/vmap()/add | solution.py:33
  348.1 32.9 %copy.489 = f32[2,16,3,16,3,16,3]{5,3,6,4,2,1,0:T(8,128)} copy(f32[2,16,3,16,3,16,3]{6,5,4,3,2,1,0:T(8,128)} %sub.175) | data formatting | bytes 1769472 | tf_op jit(solution)/shard_map/vmap()/sub | solution.py:33
  381.0 32.9 %copy.488 = f32[2,16,3,16,3,16,3]{5,3,6,4,2,1,0:T(8,128)} copy(f32[2,16,3,16,3,16,3]{6,5,4,3,2,1,0:T(8,128)} %reshape.313) | data formatting | bytes 1769472 | tf_op jit(solution)/shard_map/reshape | solution.py:100
  413.9 32.9 %copy.490 = f32[2,16,3,16,3,16,3]{5,3,6,4,2,1,0:T(8,128)} copy(f32[2,16,3,16,3,16,3]{6,5,4,3,2,1,0:T(8,128)} %reshape.314) | data formatting | bytes 1769472 | tf_op jit(solution)/shard_map/reshape | solution.py:101
  446.8 32.9 %copy.517 = f32[2,16,3,16,3,16,3]{5,3,6,4,2,1,0:T(8,128)} copy(f32[2,16,3,16,3,16,3]{6,5,4,3,2,1,0:T(8,128)} %reshape.315) | data formatting | bytes 1769472 | tf_op jit(solution)/shard_map/reshape | solution.py:102
  494.0 15.8 %add_divide_fusion.8 = (f32[2,48,48,48]{3,2,1,0:T(8,128)S(1)}, f32[2,48,48,48]{3,2,1,0:T(8,128)}, f32[2,48,48,48]{3,2,1,0:T(8,128)}, f32[2,48,48,48]{3,2,1,0:T(8...) fusion(f32[2,48,48,48]{3,2,1,0:T(8,128)} %add.569, f32[2,48,48,48]{3,2,1,0:T(8,128)} %reshape.324, ...), kind=kLoop, calls=%fused_computation.88 | loop fusion | flops 4202496 | bytes 15040512 | tf_op jit(solution)/shard_map/vmap()/div | solution.py:33
  523.4 15.0 %add_divide_fusion.7 = (f32[2,48,48,48]{3,2,1,0:T(8,128)S(1)}, f32[2,48,48,48]{3,2,1,0:T(8,128)}, f32[2,48,48,48]{3,2,1,0:T(8,128)}, f32[2,48,48,48]{3,2,1,0:T(8...) fusion(f32[2,48,48,48]{3,2,1,0:T(8,128)} %add.569, f32[2,48,48,48]{3,2,1,0:T(8,128)} %reshape.324, ...), kind=kLoop, calls=%fused_computation.87 | loop fusion | flops 4202496 | bytes 15040512 | tf_op jit(solution)/shard_map/vmap()/div | solution.py:33
  552.2 15.6 %add_divide_fusion.6 = (f32[2,48,48,48]{3,2,1,0:T(8,128)S(1)}, f32[2,48,48,48]{3,2,1,0:T(8,128)}, f32[2,48,48,48]{3,2,1,0:T(8,128)}, f32[2,48,48,48]{3,2,1,0:T(8...) fusion(f32[2,48,48,48]{3,2,1,0:T(8,128)} %add.569, f32[2,48,48,48]{3,2,1,0:T(8,128)} %reshape.324, ...), kind=kLoop, calls=%fused_computation.86 | loop fusion | flops 4202496 | bytes 15040512 | tf_op jit(solution)/shard_map/vmap()/div | solution.py:33
  567.8 24.5 %reshape.431 = f32[2,16,3,16,3,16,3]{6,5,4,3,2,1,0:T(8,128)} reshape(f32[2,48,48,48]{3,2,1,0:T(8,128)} %get-tuple-element.192) | data formatting | bytes 1769472 | tf_op jit(solution)/shard_map/vmap()/add | solution.py:32
  592.2 32.9 %copy.542 = f32[2,16,3,16,3,16,3]{5,3,6,4,2,1,0:T(8,128)} copy(f32[2,16,3,16,3,16,3]{6,5,4,3,2,1,0:T(8,128)} %reshape.431) | data formatting | bytes 1769472 | tf_op jit(solution)/shard_map/vmap()/add | solution.py:32
  625.2 24.7 %reshape.430 = f32[2,16,3,16,3,16,3]{6,5,4,3,2,1,0:T(8,128)} reshape(f32[2,48,48,48]{3,2,1,0:T(8,128)} %get-tuple-element.200) | data formatting | bytes 1769472 | tf_op jit(solution)/shard_map/vmap()/add | solution.py:32
  649.8 32.9 %copy.529 = f32[2,16,3,16,3,16,3]{5,3,6,4,2,1,0:T(8,128)} copy(f32[2,16,3,16,3,16,3]{6,5,4,3,2,1,0:T(8,128)} %reshape.430) | data formatting | bytes 1769472 | tf_op jit(solution)/shard_map/vmap()/add | solution.py:32
  682.7 24.5 %reshape.429 = f32[2,16,3,16,3,16,3]{6,5,4,3,2,1,0:T(8,128)} reshape(f32[2,48,48,48]{3,2,1,0:T(8,128)} %get-tuple-element.206) | data formatting | bytes 1769472 | tf_op jit(solution)/shard_map/vmap()/add | solution.py:32
  707.2 32.9 %copy.516 = f32[2,16,3,16,3,16,3]{5,3,6,4,2,1,0:T(8,128)} copy(f32[2,16,3,16,3,16,3]{6,5,4,3,2,1,0:T(8,128)} %reshape.429) | data formatting | bytes 1769472 | tf_op jit(solution)/shard_map/vmap()/add | solution.py:32
  740.1 22.6 %fusion.114 = (f32[2,16,16,16]{3,2,1,0:T(8,128)S(1)}, f32[2,16,3,16,3,16,3]{5,3,6,4,2,1,0:T(8,128)}) fusion(f32[2,16,3,16,3,16,3]{5,3,6,4,2,1,0:T(8,128)} %copy.518, f32[2,16,3,16,3,16,3]{5,3,6,4,2,1,0:T(8,128)} %copy.517, f32[2,16,3,16,3,16,3]{5,3,6,4,2,1,0:T(8,128)} %copy.542, f32[2,16,3,16,3,16,3]{5,3,6,4,2,1,0:T(8,128)} %copy.489, ...), kind=kLoop, calls=%fused_computation.335 | loop fusion | flops 5521408 | bytes 7995392 | tf_op jit(solution)/shard_map/reduce_sum | solution.py:131
  848.0 14.9 %while.6 = (s32[]{:T(128)}, f32[66,66,130]{2,1,0:T(8,128)}, s32[4,3]{1,0:T(4,128)S(1)}, f32[4,18,18,18]{3,2,1,0:T(8,128)S(1)}, s32[]{:T(128)}) while((s32[]{:T(128)}, f32[66,66,130]{2,1,0:T(8,128)}, s32[4,3]{1,0:T(4,128)S(1)}, f32[4,18,18,18]{3,2,1,0:T(8,128)S(1)}, s32[]{:T(128)}) %tuple.222), condition=%wide.while_cond.2, body=%wide.while_body.2.sunk | while | flops 2 | bytes 244649 | solution.py:50
  899.2 14.9 %while.7 = (s32[]{:T(128)}, f32[66,66,130]{2,1,0:T(8,128)}, s32[4,3]{1,0:T(4,128)S(1)}, f32[4,18,18,18]{3,2,1,0:T(8,128)S(1)}, s32[]{:T(128)}) while((s32[]{:T(128)}, f32[66,66,130]{2,1,0:T(8,128)}, s32[4,3]{1,0:T(4,128)S(1)}, f32[4,18,18,18]{3,2,1,0:T(8,128)S(1)}, s32[]{:T(128)}) %tuple.223), condition=%wide.while_cond.3, body=%wide.while_body.3.sunk | while | flops 2 | bytes 244649 | solution.py:50
  960.5 15.0 %add_divide_fusion.5 = (f32[2,48,48,48]{3,2,1,0:T(8,128)S(1)}, f32[2,48,48,48]{3,2,1,0:T(8,128)}, f32[2,48,48,48]{3,2,1,0:T(8,128)}, f32[2,48,48,48]{3,2,1,0:T(8...) fusion(f32[2,48,48,48]{3,2,1,0:T(8,128)} %add.569, f32[2,48,48,48]{3,2,1,0:T(8,128)} %reshape.324, ...), kind=kLoop, calls=%fused_computation.85 | loop fusion | flops 4202496 | bytes 15040512 | tf_op jit(solution)/shard_map/vmap()/div | solution.py:33
  989.0 15.2 %add_divide_fusion.4 = (f32[2,48,48,48]{3,2,1,0:T(8,128)S(1)}, f32[2,48,48,48]{3,2,1,0:T(8,128)}, f32[2,48,48,48]{3,2,1,0:T(8,128)}, f32[2,48,48,48]{3,2,1,0:T(8...) fusion(f32[2,48,48,48]{3,2,1,0:T(8,128)} %add.569, f32[2,48,48,48]{3,2,1,0:T(8,128)} %reshape.324, ...), kind=kLoop, calls=%fused_computation.84 | loop fusion | flops 4202496 | bytes 15040512 | tf_op jit(solution)/shard_map/vmap()/div | solution.py:33
  1027.2 24.5 %reshape.434 = f32[2,16,3,16,3,16,3]{6,5,4,3,2,1,0:T(8,128)} reshape(f32[2,48,48,48]{3,2,1,0:T(8,128)} %get-tuple-element.174) | data formatting | bytes 1769472 | tf_op jit(solution)/shard_map/vmap()/add | solution.py:32
  1051.6 33.1 %copy.596 = f32[2,16,3,16,3,16,3]{5,3,6,4,2,1,0:T(8,128)} copy(f32[2,16,3,16,3,16,3]{6,5,4,3,2,1,0:T(8,128)} %reshape.434) | data formatting | bytes 1769472 | tf_op jit(solution)/shard_map/vmap()/add | solution.py:32
  1084.7 23.6 %reshape.433 = f32[2,16,3,16,3,16,3]{6,5,4,3,2,1,0:T(8,128)} reshape(f32[2,48,48,48]{3,2,1,0:T(8,128)S(1)} %copy-done.15) | data formatting | bytes 1769472 | tf_op jit(solution)/shard_map/vmap()/add | solution.py:32
  1108.3 33.1 %copy.583 = f32[2,16,3,16,3,16,3]{5,3,6,4,2,1,0:T(8,128)} copy(f32[2,16,3,16,3,16,3]{6,5,4,3,2,1,0:T(8,128)} %reshape.433) | data formatting | bytes 1769472 | tf_op jit(solution)/shard_map/vmap()/add | solution.py:32
  1141.4 23.6 %reshape.432 = f32[2,16,3,16,3,16,3]{6,5,4,3,2,1,0:T(8,128)} reshape(f32[2,48,48,48]{3,2,1,0:T(8,128)S(1)} %copy-done.14) | data formatting | bytes 1769472 | tf_op jit(solution)/shard_map/vmap()/add | solution.py:32
  1164.9 32.9 %copy.570 = f32[2,16,3,16,3,16,3]{5,3,6,4,2,1,0:T(8,128)} copy(f32[2,16,3,16,3,16,3]{6,5,4,3,2,1,0:T(8,128)} %reshape.432) | data formatting | bytes 1769472 | tf_op jit(solution)/shard_map/vmap()/add | solution.py:32
  1197.8 26.4 %fusion = f32[2,16,16,16]{3,2,1,0:T(8,128)S(1)} fusion(f32[2,16,3,16,3,16,3]{5,3,6,4,2,1,0:T(8,128)} %copy.518, f32[2,16,3,16,3,16,3]{5,3,6,4,2,1,0:T(8,128)} %copy.517, f32[2,16,3,16,3,16,3]{5,3,6,4,2,1,0:T(8,128)} %copy.596, f32[2,16,3,16,3,16,3]{5,3,6,4,2,1,0:T(8,128)} %copy.489, f32[2,16,3,16,3,16,3]{5,3,6,4,2,1,0:T(8,128)} %copy.583, ...), kind=kLoop, calls=%fused_computation.14 | loop fusion | flops 9060352 | bytes 9764864 | tf_op jit(solution)/shard_map/reduce_sum | solution.py:131
  (486 shorter events, 531.0 us)
Async XLA Ops:
  1.6 7.9 collective-permute-start
  2.9 6.3 collective-permute-start.1
  6.6 297.8 %copy-start.55 = (s32[4]{0:T(128)}, s32[4]{0:T(128)S(1)}, u32[]{:S(2)}) copy-start(s32[4]{0:T(128)S(1)} %slice_bitcast_fusion.54) | copy-start | bytes 52
  10.9 214.7 %collective-permute-start.3 = (f32[66,1,128]{2,1,0:T(1,128)S(1)}, f32[66,1,128]{2,1,0:T(1,128)S(1)}, u32[]{:S(2)}, u32[]{:S(2)}) collective-permute-start(f32[66,1,128]{2,1,0:T(1,128)S(1)} %get-tuple-element.265), channel_id=1, source_target_pairs={{0,1},{1,2},{2,3},{3,4},{4,5},{5,6},{6,7},{8,9},{9,10},{10,11},{11... | collective-permute-start | bytes 101384 | tf_op jit(solution)/shard_map/ppermute | solution.py:19
  15.8 209.8 %collective-permute-start.2 = (f32[66,1,128]{2,1,0:T(1,128)S(1)}, f32[66,1,128]{2,1,0:T(1,128)S(1)}, u32[]{:S(2)}, u32[]{:S(2)}) collective-permute-start(f32[66,1,128]{2,1,0:T(1,128)S(1)} %get-tuple-element.266), channel_id=1, source_target_pairs={{1,0},{2,1},{3,2},{4,3},{5,4},{6,5},{7,6},{9,8},{10,9},{11,10},{12... | collective-permute-start | bytes 101384 | tf_op jit(solution)/shard_map/ppermute | solution.py:20
  17.1 287.3 %copy-start.58 = (s32[32,2]{0,1:T(2,128)}, s32[32,2]{0,1:T(2,128)S(1)}, u32[]{:S(2)}) copy-start(s32[32,2]{0,1:T(2,128)S(1)} %multiply_add_fusion.6) | copy-start | bytes 772
  61.7 38.7 %copy-start.31 = (f32[2,48,2304]{2,1,0:T(8,128)S(1)}, f32[2,48,2304]{2,1,0:T(8,128)}, u32[]{:S(2)}) copy-start(f32[2,48,2304]{2,1,0:T(8,128)} %param.14) | copy-start | bytes 2654212
  101.9 382.9 %copy-start.2 = (f32[2,48,48,48]{3,2,1,0:T(8,128)}, f32[2,48,48,48]{3,2,1,0:T(8,128)S(1)}, u32[]{:S(2)}) copy-start(f32[2,48,48,48]{3,2,1,0:T(8,128)S(1)} %reshape.320) | copy-start | bytes 2654212
  144.1 39.8 %copy-start.29 = (f32[2,48,2304]{2,1,0:T(8,128)S(1)}, f32[2,48,2304]{2,1,0:T(8,128)}, u32[]{:S(2)}) copy-start(f32[2,48,2304]{2,1,0:T(8,128)} %param.16) | copy-start | bytes 2654212
  258.7 22.1 %copy-start.4 = (f32[64,64,128]{2,1,0:T(8,128)}, f32[64,64,128]{2,1,0:T(8,128)S(1)}, u32[]{:S(2)}) copy-start(f32[64,64,128]{2,1,0:T(8,128)S(1)} %fusion.36) | copy-start | bytes 6291460
  258.7 5.2 collective-permute-start.4
  261.5 3.4 collective-permute-start.5
  264.9 6.7 collective-permute-start.6
  269.5 6.1 collective-permute-start.7
  306.5 181.2 %all-to-all-start = ((f32[32,2,12,256]{3,1,2,0:T(2,128)}), f32[32,2,12,256]{3,1,2,0:T(2,128)S(1)}, u32[]{:S(2)}, u32[]{:S(2)}) async-start(f32[32,2,12,256]{3,1,2,0:T(2,128)} %copy.505), calls=%async_computation | async-start | bytes 1572864 | tf_op jit(solution)/shard_map/all_to_all | solution.py:118
  315.2 172.5 %copy-start.53 = (pred[2,32,1,1]{1,2,3,0:T(4,128)(4,1)}, pred[2,32,1,1]{1,2,3,0:T(4,128)(4,1)S(1)}, u32[]{:S(2)}) copy-start(pred[2,32,1,1]{1,2,3,0:T(4,128)(4,1)S(1)} %copy.624) | copy-start | bytes 196
  740.1 22.8 %copy-start.48 = (f32[2,32]{0,1:T(8,128)S(1)}, f32[2,32]{0,1:T(8,128)}, u32[]{:S(2)}) copy-start(f32[2,32]{0,1:T(8,128)} %get-tuple-element.341) | copy-start | bytes 772
  764.4 35.2 %copy-start.56 = (s32[4]{0:T(128)S(1)}, s32[4]{0:T(128)}, u32[]{:S(2)}) copy-start(s32[4]{0:T(128)} %copy-done.55) | copy-start | bytes 52
  764.4 33.5 %all-to-all-start.1 = ((f32[32,2,4096]{2,1,0:T(2,128)}), f32[32,2,4096]{2,1,0:T(2,128)S(1)}, u32[]{:S(2)}, u32[]{:S(2)}) async-start(f32[32,2,4096]{2,1,0:T(2,128)} %multiply_bitcast_fusion.1), calls=%async_computation.1 | async-start | bytes 2097152 | tf_op jit(solution)/shard_map/all_to_all | solution.py:135
  822.4 7.0 collective-permute-start.9
  828.1 3.6 collective-permute-start.8
  832.8 4.2 collective-permute-start.11
  835.4 5.8 collective-permute-start.10
  877.5 5.3 collective-permute-start.12
  880.7 4.0 collective-permute-start.13
  884.8 5.6 collective-permute-start.14
  888.2 5.8 collective-permute-start.15
  925.2 29.1 %all-to-all-start.2 = ((f32[32,2,12,256]{3,1,2,0:T(2,128)}), f32[32,2,12,256]{3,1,2,0:T(2,128)S(1)}, u32[]{:S(2)}, u32[]{:S(2)}) async-start(f32[32,2,12,256]{3,1,2,0:T(2,128)} %copy.560), calls=%async_computation.2 | async-start | bytes 1572864 | tf_op jit(solution)/shard_map/all_to_all | solution.py:118
  1051.6 33.1 %copy-start.15 = (f32[2,48,48,48]{3,2,1,0:T(8,128)S(1)}, f32[2,48,48,48]{3,2,1,0:T(8,128)}, u32[]{:S(2)}) copy-start(f32[2,48,48,48]{3,2,1,0:T(8,128)} %get-tuple-element.180) | copy-start | bytes 2654212
  1108.3 33.1 %copy-start.14 = (f32[2,48,48,48]{3,2,1,0:T(8,128)S(1)}, f32[2,48,48,48]{3,2,1,0:T(8,128)}, u32[]{:S(2)}) copy-start(f32[2,48,48,48]{3,2,1,0:T(8,128)} %get-tuple-element.186) | copy-start | bytes 2654212
  1197.8 26.6 %copy-start.49 = (f32[2,32]{0,1:T(8,128)S(1)}, f32[2,32]{0,1:T(8,128)}, u32[]{:S(2)}) copy-start(f32[2,32]{0,1:T(8,128)} %get-tuple-element.341) | copy-start | bytes 772
  1226.0 120.4 %all-to-all-start.3 = ((f32[32,2,4096]{2,1,0:T(2,128)}), f32[32,2,4096]{2,1,0:T(2,128)}, u32[]{:S(2)}, u32[]{:S(2)}) async-start(f32[32,2,4096]{2,1,0:T(2,128)} %multiply_bitcast_fusion), calls=%async_computation.3 | async-start | bytes 2097152 | tf_op jit(solution)/shard_map/all_to_all | solution.py:135
  (52 other events, 289.9 us)
where the time goes:
time: 1390 us; the launch traced here: 1370 us
  local copies, waits for them, and re-layouts  1020 us (73%)
  other arithmetic  217 us (16%)
  starting transfers between devices  64.7 us (5%)
  waiting for transfers between devices  34.6 us (2%)
  between operations  24.7 us (2%)
    add x12, local copies, waits for them, and re-layouts, fine_update(): lap = xm + xp + ym + yp + zm + zp - 6.0 * field  343 us
    div x6, other arithmetic, fine_update(): (2.0 * field - (1.0 - absorb) * before + courant * lap) / (1.0 + absorb)  90.6 us
    reshape x3, local copies, waits for them, and re-layouts, on_device(): fine_prev = fine_before.reshape(shape)  76.2 us
    add x3, local copies, waits for them, and re-layouts, fine_update(): 1.0 + absorb  74.6 us
    sub x3, local copies, waits for them, and re-layouts, fine_update(): 1.0 - absorb  74.6 us
    reshape x3, local copies, waits for them, and re-layouts, on_device(): fine_c = fine_courant.reshape(shape)  74.5 us
    reshape x3, local copies, waits for them, and re-layouts, on_device(): fine = fine_now.reshape(shape)  73 us
    gather x48, local copies, waits for them, and re-layouts  59.1 us
  transfers between devices with their start and end apart: 20, of which 9 were waited for; matrix products, arithmetic and copies ran while one was open for 38% of the time, Pallas kernels for 0%

commit v1 on v0

v1 whole, which is shorter than its diff:
```python
import functools

import jax
import jax.numpy as jnp
import ml_dtypes
import numpy as np
from jax import lax
from jax.experimental import pallas as pl
from jax.experimental.pallas import tpu as pltpu
from jax.sharding import PartitionSpec as P

STEPS = 2
MESH = pl.DeviceIdType.MESH
BC, FINE = 16, 48
ROW = FINE * FINE
EDGE = 128
bf16 = jnp.bfloat16


def constants():
    flat = np.arange(ROW)
    y, z = flat // FINE, flat % FINE
    group = np.arange(BC)[:, None]
    spread = np.zeros((128, ROW), np.float32)
    spread[0:16] = (y == 0) & (z // 3 == group)
    spread[16:32] = (y == FINE - 1) & (z // 3 == group)
    spread[32:48] = (z == 0) & (y // 3 == group)
    spread[48:64] = (z == FINE - 1) & (y // 3 == group)
    spread[64:80] = z // 3 == group
    spread = np.concatenate([spread, spread], 0)
    up = np.zeros((160, 96), np.float32)
    for box in range(2):
        for x in range(FINE):
            up[box * 48 + x, box * 48 + x // 3] = 1
        for r in range(32):
            up[96 + box * 32 + r, box * 48 + 16 + r] = 1
    rows = (y // 3 == group).astype(np.float32)
    inside = np.stack([np.tile(z != 0, (8, 1)), np.tile(z != FINE - 1, (8, 1))]).astype(np.float32)
    down = np.zeros((16, 96), np.float32)
    for x in range(FINE):
        down[x // 3, x] = 1
        down[x // 3, 48 + x] = 1
    gather = np.zeros((ROW, 256), np.float32)
    gather[flat, (y // 3) * 16 + z // 3] = 1
    rep = np.zeros((256, 16), np.float32)
    rep[np.arange(256), np.arange(256) // 16] = 1
    own = (np.arange(256)[:, None] % 16 == np.arange(256)[None] // 16).astype(np.float32)
    tile = (np.arange(256)[:, None] % 16 == np.arange(128)[None] % 16).astype(np.float32)
    tile = np.concatenate([tile, tile], 0)
    half = ml_dtypes.bfloat16
    return [
        spread.astype(half), up.astype(half), rows, inside, down.astype(half),
        gather.astype(half), rep.astype(half), own, tile.astype(half),
    ]


def split(value):
    high = value.astype(bf16)
    low = (value - high.astype(jnp.float32)).astype(bf16)
    return high, low


def dot(a, b):
    return jnp.dot(a, b, preferred_element_type=jnp.float32)


def kernel(
    nt, nb,
    inter, anchor,
    now_h, before_h, courant_h, absorb_h, fnow_h, fbefore_h, fcourant_h, fabsorb_h,
    spread, up, rows, inside, down, gather, rep, own, tile,
    next_h, last_h, fnext_h, flast_h,
    p0, p1, p2, q0, rc, r2, fa, fb, frc, fr2,
    halo_out, halo_in, face_out, face_in, rest_out, rest_in,
    ghost, blocks, cubes, edges,
    halo_ss, halo_rs, face_ss, face_rs, rest_ss, rest_rs, load_sem, store_sem,
):
    t, b = lax.axis_index("tile"), lax.axis_index("bulk")
    fields = [p0, p1, p2]
    nx, ny = 64, 64

    exists = [t > 0, t < nt - 1, b > 0, b < nb - 1]
    missing = [t == 0, t == nt - 1, b == 0, b == nb - 1]
    beside = [(t - 1, b), (t + 1, b), (t, b - 1), (t, b + 1)]
    b_other = b + 1 - 2 * lax.rem(b, 2)
    t_other = lax.rem(t + nt // 2, nt)
    quad = [(t, b), (t, b_other), (t_other, b), (t_other, b_other)]

    mid = (pl.ds(1, nx), pl.ds(8, ny), slice(None))
    fmid = (slice(None), pl.ds(8, FINE), pl.ds(EDGE, ROW))
    loads = [
        pltpu.make_async_copy(src, dst, load_sem.at[i])
        for i, (src, dst) in enumerate([
            (now_h, p0.at[mid]),
            (before_h, q0),
            (courant_h, rc),
            (absorb_h, r2),
            (fnow_h, fa.at[fmid]),
            (fbefore_h, fb.at[fmid]),
            (fcourant_h, frc),
            (fabsorb_h, fr2),
        ])
    ]
    for load in loads:
        load.start()

    barrier = pltpu.get_barrier_semaphore()
    for have, device in zip(exists, beside):
        @pl.when(have)
        def _(device=device):
            pl.semaphore_signal(barrier, inc=1, device_id=device, device_id_type=MESH)
    for device in quad[2:]:
        pl.semaphore_signal(barrier, inc=1, device_id=device, device_id_type=MESH)
    peers = jnp.int32(2)
    for have in exists:
        peers = peers + jnp.where(have, 1, 0)
    pl.semaphore_wait(barrier, peers)

    zero_side = jnp.zeros((2, 64, EDGE), jnp.float32)
    for buf in (fa, fb):
        buf[:, :, pl.ds(0, EDGE)] = zero_side
        buf[:, :, pl.ds(EDGE + ROW, EDGE)] = zero_side

    lane = lax.broadcasted_iota(jnp.int32, (64, 128), 1)
    not_first, not_last = lane != 0, lane != 127

    def halo_wait(phase, side):
        return pltpu.make_async_remote_copy(
            src_ref=halo_out.at[phase, side],
            dst_ref=halo_in.at[phase, side],
            send_sem=halo_ss.at[phase, side],
            recv_sem=halo_rs.at[phase, side],
            device_id=beside[side],
            device_id_type=MESH,
        )

    def halo_copy(phase, side):
        return pltpu.make_async_remote_copy(
            src_ref=halo_out.at[phase, side],
            dst_ref=halo_in.at[phase, side ^ 1],
            send_sem=halo_ss.at[phase, side],
            recv_sem=halo_rs.at[phase, side ^ 1],
            device_id=beside[side],
            device_id_type=MESH,
        )

    def send_halo(phase, field):
        halo_out[phase, 0] = field[1, pl.ds(8, ny), :]
        halo_out[phase, 1] = field[nx, pl.ds(8, ny), :]
        halo_out[phase, 2] = field[pl.ds(1, nx), 8, :]
        halo_out[phase, 3] = field[pl.ds(1, nx), 7 + ny, :]
        for side in range(4):
            @pl.when(exists[side])
            def _(side=side):
                halo_copy(phase, side).start()

    def take_halo(phase, field):
        for side in range(4):
            @pl.when(exists[side])
            def _(side=side):
                halo_wait(phase, side).wait_recv()

            @pl.when(missing[side])
            def _(side=side):
                halo_in[phase, side] = jnp.zeros((64, 128), jnp.float32)
        field[0, pl.ds(8, ny), :] = halo_in[phase, 0]
        field[nx + 1, pl.ds(8, ny), :] = halo_in[phase, 1]
        field[pl.ds(1, nx), 7, :] = halo_in[phase, 2]
        field[pl.ds(1, nx), 8 + ny, :] = halo_in[phase, 3]

    def face_copy(phase, j):
        return pltpu.make_async_remote_copy(
            src_ref=face_out.at[phase, j - 1],
            dst_ref=face_in.at[phase, j],
            send_sem=face_ss.at[phase, j - 1],
            recv_sem=face_rs.at[phase, j - 1],
            device_id=quad[j],
            device_id_type=MESH,
        )

    def rest_copy(step, j):
        return pltpu.make_async_remote_copy(
            src_ref=rest_out.at[step],
            dst_ref=rest_in.at[step, j],
            send_sem=rest_ss.at[step, j - 1],
            recv_sem=rest_rs.at[step, j - 1],
            device_id=quad[j],
            device_id_type=MESH,
        )

    lane16 = lax.broadcasted_iota(jnp.int32, (16, 128), 1)
    z_in = lax.broadcasted_iota(jnp.int32, (256, 128), 0)
    z_in = lax.rem(z_in, 128)
    z_out = lax.broadcasted_iota(jnp.int32, (256, 128), 1)
    y_row = lax.broadcasted_iota(jnp.int32, (16, 16, 128), 1)
    y_lane = lax.rem(lax.broadcasted_iota(jnp.int32, (16, 16, 128), 2), 16)

    def collect(field):
        at = [4 * lax.div(inter[0, 1, e], 16) + lax.div(inter[0, 2, e], 16) for e in range(4)]
        spots = [jnp.full((16, 128), a, jnp.int32) for a in at]

        def choose(load, height, store):
            values = [None] * 4
            for i in range(4):
                for j in range(4):
                    value = load(i, j)
                    for e in range(4):
                        if i + j == 0:
                            values[e] = value
                        else:
                            values[e] = jnp.where(spots[e][:height] == 4 * i + j, value, values[e])
            for e in range(4):
                store(e, values[e])

        def to_edges(row, height):
            def store(e, value):
                edges[e, pl.ds(row, height), :] = value
            return store

        choose(lambda i, j: field[16 * i, pl.ds(8 + 16 * j, 16), :], 16, to_edges(32, 16))
        choose(lambda i, j: field[16 * i + 17, pl.ds(8 + 16 * j, 16), :], 16, to_edges(48, 16))

        @pl.loop(0, 16)
        def _(u):
            def to_cubes(e, value):
                cubes[e, pl.ds(pl.multiple_of(16 * u, 16), 16), :] = value
            choose(lambda i, j: field[16 * i + 1 + u, pl.ds(8 + 16 * j, 16), :], 16, to_cubes)
            choose(lambda i, j: field[16 * i + 1 + u, pl.ds(7 + 16 * j, 1), :], 1, to_edges(u, 1))
            choose(lambda i, j: field[16 * i + 1 + u, pl.ds(24 + 16 * j, 1), :], 1, to_edges(16 + u, 1))

    def faces_of(ref, entry):
        z0 = inter[0, 3, entry]
        high, low = split(cubes[entry])
        pick = ((z_in == z0 - 1) & (z_out >= 32) & (z_out < 48)) | (
            (z_in == z0 + 16) & (z_out >= 48) & (z_out < 64)
        )
        pick = jnp.where(pick, 1.0, 0.0).astype(bf16)
        zs = dot(jnp.concatenate([high, low], axis=1), pick).reshape(16, 16, 128)
        zs = jnp.sum(jnp.where(y_row == y_lane, zs, 0.0), axis=1)
        high, low = split(edges[entry])
        window = jnp.where(z_in == z0 + lax.rem(z_out, 16), 1.0, 0.0).astype(bf16)
        flat = dot(jnp.concatenate([high, low], axis=1), window)
        first = jnp.where(lane16 < 16, flat[0:16], jnp.where(lane16 < 32, flat[16:32], zs))
        x_lanes = (lane16 >= 64) & (lane16 < 80)
        ref[pl.ds(0, 16), :] = jnp.where(lane16 < 64, first, 0.0)
        ref[pl.ds(16, 16), :] = jnp.where(x_lanes, flat[32:48], 0.0)
        ref[pl.ds(32, 16), :] = jnp.where(x_lanes, flat[48:64], 0.0)

    def faces_for(j, slot):
        target = 2 * (quad[j][0] * nb + quad[j][1]) + slot
        value = blocks[0, pl.ds(0, 48), :]
        for entry in range(1, 4):
            hit = inter[0, 0, entry] == target
            value = jnp.where(hit, blocks[entry, pl.ds(0, 48), :], value)
        return value

    def send_faces(phase, field):
        collect(field)

        @pl.loop(0, 4)
        def _(entry):
            faces_of(blocks.at[entry, pl.ds(0, 48), :], entry)
        for j in range(1, 4):
            for slot in range(2):
                face_out[phase, j - 1, slot] = faces_for(j, slot)
            face_copy(phase, j).start()
        for slot in range(2):
            face_in[phase, 0, slot] = faces_for(0, slot)

    def take_faces(phase):
        for j in range(1, 4):
            face_copy(phase, j).wait_recv()

    def source_of(slot):
        away_t = jnp.where(lax.div(anchor[slot, 0], 64) == t, 0, 2)
        away_b = jnp.where(lax.div(anchor[slot, 1], 64) == b, 0, 1)
        return away_t + away_b

    sources = [source_of(slot) for slot in range(2)]

    def arrived(phase, slot):
        value = face_in[phase, 0, slot]
        for j in range(1, 4):
            value = jnp.where(sources[slot] == j, face_in[phase, j, slot], value)
        return value

    def coarse_update(new, field, before):
        @pl.loop(0, nx)
        def _(x):
            c = field[x + 1, pl.ds(8, ny), :]
            nbs = field[x, pl.ds(8, ny), :] + field[x + 2, pl.ds(8, ny), :]
            nbs = nbs + field[x + 1, pl.ds(7, ny), :] + field[x + 1, pl.ds(9, ny), :]
            nbs = nbs + jnp.where(not_first, pltpu.roll(c, 1, 1), 0.0)
            nbs = nbs + jnp.where(not_last, pltpu.roll(c, 127, 1), 0.0)
            old = before(x)
            new[x + 1, pl.ds(8, ny), :] = old + r2[x] * (c - old) + rc[x] * (nbs - 6.0 * c)

    row = lax.broadcasted_iota(jnp.int32, (8, ROW), 0)

    def make_ghosts(f, phase, weight):
        parts = []
        for slot in range(2):
            q = arrived(2 * phase, slot)
            if weight:
                q = q + weight * (arrived(2 * phase + 1, slot) - q)
            parts.append(q)
        high, low = split(jnp.concatenate(parts, axis=0))
        left = dot(up[...], jnp.concatenate([high, low], axis=1)).astype(bf16)

        @pl.loop(0, 9)
        def _(c):
            cols = pl.ds(pl.multiple_of(c * 256, 256), 256)
            ghost[:, cols] = dot(left, spread[:, cols])
        for slot in range(2):
            for k in range(2):
                face = ghost[pl.ds(96 + 32 * slot + 16 * k, 16), :] * rows[...]
                f[slot, pl.ds(7 + 49 * k, 1), pl.ds(EDGE, ROW)] = jnp.sum(face, axis=0, keepdims=True)

    def fine_update(f, g, slot):
        @pl.loop(0, 6)
        def _(i):
            base = pl.multiple_of(8 * i, 8)
            prev = f[slot, pl.ds(base, 8), pl.ds(EDGE, ROW)]
            after = f[slot, pl.ds(pl.multiple_of(base + 16, 8), 8), pl.ds(EDGE, ROW)]
            wide = f[slot, pl.ds(pl.multiple_of(base + 8, 8), 8), :]
            c = wide[:, EDGE:EDGE + ROW]
            width = ROW + 2 * EDGE
            nbs = jnp.where(row == 0, pltpu.roll(prev, 1, 0), pltpu.roll(c, 1, 0))
            nbs = nbs + jnp.where(row == 7, pltpu.roll(after, 7, 0), pltpu.roll(c, 7, 0))
            nbs = nbs + pltpu.roll(wide, FINE, 1)[:, EDGE:EDGE + ROW]
            nbs = nbs + pltpu.roll(wide, width - FINE, 1)[:, EDGE:EDGE + ROW]
            nbs = nbs + pltpu.roll(wide, 1, 1)[:, EDGE:EDGE + ROW] * inside[0]
            nbs = nbs + pltpu.roll(wide, width - 1, 1)[:, EDGE:EDGE + ROW] * inside[1]
            nbs = nbs + ghost[pl.ds(pl.multiple_of(48 * slot + base, 8), 8), :]
            here = (slot, pl.ds(pl.multiple_of(base + 8, 8), 8), pl.ds(EDGE, ROW))
            old = g[here]
            rows_here = pl.ds(base, 8)
            g[here] = old + fr2[slot, rows_here, :] * (c - old) + frc[slot, rows_here, :] * (nbs - 6.0 * c)

    def restrict(f, step):
        lefts = []
        for slot in range(2):
            high, low = split(f[slot, pl.ds(8, FINE), pl.ds(EDGE, ROW)])
            part = dot(down[...], jnp.concatenate([high, low], axis=0))
            lefts.extend(split(part))
        means = dot(jnp.concatenate(lefts, axis=0), gather[...])
        for slot in range(2):
            mean = (means[32 * slot:32 * slot + 16] + means[32 * slot + 16:32 * slot + 32]) * (1.0 / 27.0)
            rest_out[step, slot] = mean
            rest_in[step, 0, slot] = mean
        for j in range(1, 4):
            rest_copy(step, j).start()

    def insert(new, step):
        for j in range(1, 4):
            rest_copy(step, j).wait_recv()

        @pl.loop(0, 4)
        def _(entry):
            value = rest_in[step, 0, 0]
            for j in range(4):
                for slot in range(2):
                    hit = inter[0, 0, entry] == 2 * (quad[j][0] * nb + quad[j][1]) + slot
                    value = jnp.where(hit, rest_in[step, j, slot], value)
            high, low = split(value)
            left = [(dot(rep[...], part) * own[...]).astype(bf16) for part in (high, low)]
            blocks[entry] = dot(jnp.concatenate(left, axis=1), tile[...])

        place = lax.div(lane16, 16)

        @pl.loop(0, 4)
        def _(i):
            for j in range(4):
                masks = []
                for entry in range(4):
                    hit = (inter[0, 0, entry] >= 0) & (inter[0, 1, entry] == 16 * i) & (inter[0, 2, entry] == 16 * j)
                    at = jnp.where(hit, lax.div(inter[0, 3, entry], 16), -1)
                    masks.append(place == at)

                @pl.loop(0, 16)
                def _(x):
                    where = (16 * i + x + 1, pl.ds(8 + 16 * j, 16), slice(None))
                    value = new[where]
                    for entry in range(4):
                        block = blocks[entry, pl.ds(pl.multiple_of(16 * x, 16), 16), :]
                        value = jnp.where(masks[entry], block, value)
                    new[where] = value

    loads[0].wait()
    send_halo(0, p0)
    for load in loads[1:]:
        load.wait()

    @pl.loop(0, nx)
    def _(x):
        r = 1.0 / (1.0 + r2[x])
        r2[x] = 2.0 * r
        rc[x] = rc[x] * r

    for slot in range(2):
        @pl.loop(0, 6)
        def _(i):
            at = (slot, pl.ds(pl.multiple_of(8 * i, 8), 8), slice(None))
            r = 1.0 / (1.0 + fr2[at])
            fr2[at] = 2.0 * r
            frc[at] = frc[at] * r

    f, g = fa, fb
    stores = []
    for step in range(STEPS):
        field, new = fields[step], fields[step + 1]
        if step == 0:
            def before(x):
                return q0[x]
        else:
            def before(x):
                return p0[x + 1, pl.ds(8, ny), :]
            send_halo(2, field)
        take_halo(2 * step, field)
        send_faces(2 * step, field)
        coarse_update(new, field, before)
        send_halo(2 * step + 1, new)
        take_faces(2 * step)
        make_ghosts(f, step, 0.0)
        fine_update(f, g, 0)
        take_halo(2 * step + 1, new)
        send_faces(2 * step + 1, new)
        fine_update(f, g, 1)
        f, g = g, f
        take_faces(2 * step + 1)
        for sub in (1, 2):
            make_ghosts(f, step, sub / 3.0)
            for slot in range(2):
                fine_update(f, g, slot)
            f, g = g, f
        restrict(f, step)
        if step == STEPS - 1:
            stores.append(pltpu.make_async_copy(f.at[fmid], fnext_h, store_sem.at[0]))
            stores.append(pltpu.make_async_copy(g.at[fmid], flast_h, store_sem.at[1]))
            for store in stores[-2:]:
                store.start()
        insert(new, step)
        out = next_h if step == STEPS - 1 else last_h
        store = pltpu.make_async_copy(new.at[mid], out, store_sem.at[2 + step])
        if step == STEPS - 1:
            store.start()
            stores.append(store)
        else:
            last_store = store
            last_store.start()

    for phase in range(4):
        for side in range(4):
            @pl.when(exists[side])
            def _(phase=phase, side=side):
                halo_copy(phase, side).wait_send()
        for j in range(1, 4):
            face_copy(phase, j).wait_send()
    for step in range(STEPS):
        for j in range(1, 4):
            rest_copy(step, j).wait_send()
    last_store.wait()
    for store in stores:
        store.wait()


def on_device(nt, nb, *args):
    coarse, fine = args[:4], args[4:8]
    anchor, inter = args[8], args[9]
    consts = [jnp.asarray(c) for c in constants()]
    f32 = jnp.float32
    smem = pl.BlockSpec(memory_space=pltpu.SMEM)
    vmem = pl.BlockSpec(memory_space=pltpu.VMEM)
    hbm = pl.BlockSpec(memory_space=pl.ANY)
    shape_c, shape_f = coarse[0].shape, fine[0].shape
    dma = pltpu.SemaphoreType.DMA
    return pl.pallas_call(
        functools.partial(kernel, nt, nb),
        out_shape=[jax.ShapeDtypeStruct(s, f32) for s in (shape_c, shape_c, shape_f, shape_f)],
        in_specs=[smem, smem] + [hbm] * 8 + [vmem] * len(consts),
        out_specs=[hbm] * 4,
        scratch_shapes=[
            pltpu.VMEM((66, 80, 128), f32),
            pltpu.VMEM((66, 80, 128), f32),
            pltpu.VMEM((66, 80, 128), f32),
            pltpu.VMEM((64, 64, 128), f32),
            pltpu.VMEM((64, 64, 128), f32),
            pltpu.VMEM((64, 64, 128), f32),
            pltpu.VMEM((2, 64, ROW + 2 * EDGE), f32),
            pltpu.VMEM((2, 64, ROW + 2 * EDGE), f32),
            pltpu.VMEM((2, FINE, ROW), f32),
            pltpu.VMEM((2, FINE, ROW), f32),
            pltpu.VMEM((4, 4, 64, 128), f32),
            pltpu.VMEM((4, 4, 64, 128), f32),
            pltpu.VMEM((4, 3, 2, 48, 128), f32),
            pltpu.VMEM((4, 4, 2, 48, 128), f32),
            pltpu.VMEM((2, 2, 16, 256), f32),
            pltpu.VMEM((2, 4, 2, 16, 256), f32),
            pltpu.VMEM((160, ROW), f32),
            pltpu.VMEM((4, 256, 128), f32),
            pltpu.VMEM((4, 256, 128), f32),
            pltpu.VMEM((4, 64, 128), f32),
            dma((4, 4)), dma((4, 4)), dma((4, 3)), dma((4, 3)), dma((2, 3)), dma((2, 3)),
            dma((8,)), dma((4,)),
        ],
        compiler_params=pltpu.CompilerParams(
            collective_id=0, has_side_effects=True, vmem_limit_bytes=56 * 1024 * 1024
        ),
        cost_estimate=pl.CostEstimate(flops=40_000_000, bytes_accessed=20_000_000, transcendentals=0),
        name="wave",
    )(inter, anchor, *coarse, *fine, *consts)


def solution(mesh):
    whole = ("tile", "bulk")
    c, f = P("tile", "bulk", None), P(whole, None, None)
    return jax.shard_map(
        functools.partial(on_device, mesh.shape["tile"], mesh.shape["bulk"]),
        mesh=mesh,
        in_specs=(c, c, c, c, f, f, f, f, P(whole, None), f),
        out_specs=(c, c, f, f),
        check_vma=False,
    )
```

time: 1390 us -> 89.7 us (0.06); the launches traced: 1370 us -> 89.5 us
  local copies, waits for them, and re-layouts: 1020 us -> 6.92 us
  other arithmetic: 217 us -> 0 us
  Pallas kernels: 0 us -> 81.9 us
  starting transfers between devices: 64.7 us -> 0 us
  waiting for transfers between devices: 34.6 us -> 0 us
  between operations: 24.7 us -> 0.65 us
    add x21 -> x0, local copies, waits for them, and re-layouts: 418 us -> none  [the longest x12 343 us: fine_update(): lap = xm + xp + ym + yp + zm + zp - 6.0 * field]
    reshape x21 -> x0, local copies, waits for them, and re-layouts: 229 us -> none  [the longest x3 76.2 us: on_device(): fine_prev = fine_before.reshape(shape)]
    div x10 -> x0, other arithmetic: 113 us -> none  [the longest x6 90.6 us: fine_update(): (2.0 * field - (1.0 - absorb) * before + courant * lap) / (1.0 + absorb)]
    concatenate x49 -> x0, local copies, waits for them, and re-layouts: 102 us -> none  [the longest x12 22.7 us: fine_update(): xm = jnp.concatenate([ghosts[0][None], field[:-1]], 0)]
    pallas_call x0 -> x1, Pallas kernels: none -> 81.9 us  [on_device(): pl.pallas_call(functools.partial(kernel, nt, nb), out_shape=[jax.ShapeDty...]
    sub x3 -> x0, local copies, waits for them, and re-layouts: 74.6 us -> none  [fine_update(): 1.0 - absorb]
    gather x56 -> x0, local copies, waits for them, and re-layouts: 67.2 us -> none
    slice x51 -> x0, local copies, waits for them, and re-layouts: 53 us -> none  [the longest x6 17.4 us: fine_update(): zp = jnp.concatenate([field[:, :, 1:], ghosts[5][:, :, None]], 2)]
  transfers between devices with their start and end apart: 20 -> 0, of which waited for: 9 -> 0; matrix products, arithmetic and copies ran while one was open for 38% -> 0% of each run, Pallas kernels for 0% -> 0%
where the time goes in v1:
time: 89.7 us; the launch traced here: 89.5 us
  Pallas kernels  81.9 us (91%)
  local copies, waits for them, and re-layouts  6.92 us (8%)
    pallas_call x1, Pallas kernels, on_device(): pl.pallas_call(functools.partial(kernel, nt, nb), out_shape=[jax.ShapeDty...  81.9 us
    unnamed x10, local copies, waits for them, and re-layouts  6.92 us

profile of v1, /device:TPU:0, one launch (start us, length us, event | category | flops | bytes accessed | tf_op | source)
XLA Modules:
  0.0 89.5 jit_solution(9799477244339544077)
XLA Ops:
  0.6 81.9 %wave.1 = (f32[64,64,128]{2,1,0:T(8,128)}, f32[64,64,128]{2,1,0:T(8,128)}, f32[2,48,2304]{2,1,0:T(8,128)}, f32[2,48,2304]{2,1,0:T(8,128)}) custom-call(s32[1,4,4]{2,1,0:T(4,128)} %inter.1, s32[2,3]{1,0:T(2,128)} %anchor.1, f32[64,64,128]{2,1,0:T(8,128)} %now_h.1, f32[64,64,128]{2,1,0:T(8,128)} %before_h.1, f32[64,64,128]{2,1,0:T(8,128)} %courant_h.1, ...), custom_call_target="tpu_custom_call" | custom-call | flops 40000000 | bytes 20000000 | tf_op jit(solution)/shard_map/wave/pallas_call | solution.py:477
  82.5 0.0 copy-start
  82.6 3.3 %copy.27 = f32[64,64,128]{2,1,0:T(8,128)} copy(f32[64,64,128]{2,1,0:T(8,128)} %get-tuple-element.8) | data formatting | bytes 4194304
  85.9 0.0 copy-done
  85.9 0.0 copy-start.2
  85.9 0.0 copy-start.1
  85.9 1.3 %copy.28 = f32[64,64,128]{2,1,0:T(8,128)} copy(f32[64,64,128]{2,1,0:T(8,128)S(1)} %copy-done) | data formatting | bytes 4194304
  87.2 0.5 copy-done.2
  87.7 0.9 %copy.29 = f32[2,48,2304]{2,1,0:T(8,128)} copy(f32[2,48,2304]{2,1,0:T(8,128)S(1)} %copy-done.2) | data formatting | bytes 1769472
  88.6 0.0 copy-done.1
  88.6 0.9 %copy.30 = f32[2,48,2304]{2,1,0:T(8,128)} copy(f32[2,48,2304]{2,1,0:T(8,128)S(1)} %copy-done.1) | data formatting | bytes 1769472
Async XLA Ops:
  82.5 3.3 %copy-start = (f32[64,64,128]{2,1,0:T(8,128)S(1)}, f32[64,64,128]{2,1,0:T(8,128)}, u32[]{:S(2)}) copy-start(f32[64,64,128]{2,1,0:T(8,128)} %get-tuple-element.9) | copy-start | bytes 6291460
  85.9 1.8 %copy-start.2 = (f32[2,48,2304]{2,1,0:T(8,128)S(1)}, f32[2,48,2304]{2,1,0:T(8,128)}, u32[]{:S(2)}) copy-start(f32[2,48,2304]{2,1,0:T(8,128)} %get-tuple-element.10) | copy-start | bytes 2654212
  85.9 2.7 %copy-start.1 = (f32[2,48,2304]{2,1,0:T(8,128)S(1)}, f32[2,48,2304]{2,1,0:T(8,128)}, u32[]{:S(2)}) copy-start(f32[2,48,2304]{2,1,0:T(8,128)} %get-tuple-element.11) | copy-start | bytes 2654212

commit v2 on v1

--- a/solution.py
+++ b/solution.py
@@ -13,7 +13,7 @@
 MESH = pl.DeviceIdType.MESH
 BC, FINE = 16, 48
 ROW = FINE * FINE
-EDGE = 128
+COLS = ROW // 128
 bf16 = jnp.bfloat16
 
 
@@ -35,7 +35,9 @@
         for r in range(32):
             up[96 + box * 32 + r, box * 48 + 16 + r] = 1
     rows = (y // 3 == group).astype(np.float32)
+    rows = rows.reshape(BC, COLS, 128).transpose(1, 0, 2)
     inside = np.stack([np.tile(z != 0, (8, 1)), np.tile(z != FINE - 1, (8, 1))]).astype(np.float32)
+    inside = inside.reshape(2, 8, COLS, 128)[:, :, :3].transpose(2, 0, 1, 3)
     down = np.zeros((16, 96), np.float32)
     for x in range(FINE):
         down[x // 3, x] = 1
@@ -72,7 +74,7 @@
     next_h, last_h, fnext_h, flast_h,
     p0, p1, p2, q0, rc, r2, fa, fb, frc, fr2,
     halo_out, halo_in, face_out, face_in, rest_out, rest_in,
-    ghost, blocks, cubes, edges,
+    ghost, blocks, cubes, edges, picks, windows,
     halo_ss, halo_rs, face_ss, face_rs, rest_ss, rest_rs, load_sem, store_sem,
 ):
     t, b = lax.axis_index("tile"), lax.axis_index("bulk")
@@ -87,7 +89,6 @@
     quad = [(t, b), (t, b_other), (t_other, b), (t_other, b_other)]
 
     mid = (pl.ds(1, nx), pl.ds(8, ny), slice(None))
-    fmid = (slice(None), pl.ds(8, FINE), pl.ds(EDGE, ROW))
     loads = [
         pltpu.make_async_copy(src, dst, load_sem.at[i])
         for i, (src, dst) in enumerate([
@@ -95,10 +96,15 @@
             (before_h, q0),
             (courant_h, rc),
             (absorb_h, r2),
-            (fnow_h, fa.at[fmid]),
-            (fbefore_h, fb.at[fmid]),
-            (fcourant_h, frc),
-            (fabsorb_h, fr2),
+        ] + [
+            (src.at[:, :, pl.ds(128 * c, 128)], dst)
+            for c in range(COLS)
+            for src, dst in (
+                (fcourant_h, frc.at[:, c]),
+                (fabsorb_h, fr2.at[:, c]),
+                (fnow_h, fa.at[:, c + 1, pl.ds(8, FINE), :]),
+                (fbefore_h, fb.at[:, c + 1, pl.ds(8, FINE), :]),
+            )
         ])
     ]
     for load in loads:
@@ -116,10 +122,10 @@
         peers = peers + jnp.where(have, 1, 0)
     pl.semaphore_wait(barrier, peers)
 
-    zero_side = jnp.zeros((2, 64, EDGE), jnp.float32)
+    zero_side = jnp.zeros((2, 64, 128), jnp.float32)
     for buf in (fa, fb):
-        buf[:, :, pl.ds(0, EDGE)] = zero_side
-        buf[:, :, pl.ds(EDGE + ROW, EDGE)] = zero_side
+        buf[:, 0] = zero_side
+        buf[:, COLS + 1] = zero_side
 
     lane = lax.broadcasted_iota(jnp.int32, (64, 128), 1)
     not_first, not_last = lane != 0, lane != 127
@@ -195,23 +201,23 @@
     y_row = lax.broadcasted_iota(jnp.int32, (16, 16, 128), 1)
     y_lane = lax.rem(lax.broadcasted_iota(jnp.int32, (16, 16, 128), 2), 16)
 
+    at = [4 * lax.div(inter[0, 1, e], 16) + lax.div(inter[0, 2, e], 16) for e in range(4)]
+    spots = [jnp.full((16, 128), a, jnp.int32) for a in at]
+
+    def choose(load, height, store):
+        values = [None] * 4
+        for i in range(4):
+            for j in range(4):
+                value = load(i, j)
+                for e in range(4):
+                    if i + j == 0:
+                        values[e] = value
+                    else:
+                        values[e] = jnp.where(spots[e][:height] == 4 * i + j, value, values[e])
+        for e in range(4):
+            store(e, values[e])
+
     def collect(field):
-        at = [4 * lax.div(inter[0, 1, e], 16) + lax.div(inter[0, 2, e], 16) for e in range(4)]
-        spots = [jnp.full((16, 128), a, jnp.int32) for a in at]
-
-        def choose(load, height, store):
-            values = [None] * 4
-            for i in range(4):
-                for j in range(4):
-                    value = load(i, j)
-                    for e in range(4):
-                        if i + j == 0:
-                            values[e] = value
-                        else:
-                            values[e] = jnp.where(spots[e][:height] == 4 * i + j, value, values[e])
-            for e in range(4):
-                store(e, values[e])
-
         def to_edges(row, height):
             def store(e, value):
                 edges[e, pl.ds(row, height), :] = value
@@ -220,26 +226,36 @@
         choose(lambda i, j: field[16 * i, pl.ds(8 + 16 * j, 16), :], 16, to_edges(32, 16))
         choose(lambda i, j: field[16 * i + 17, pl.ds(8 + 16 * j, 16), :], 16, to_edges(48, 16))
 
+        choose(lambda i, j: field[pl.ds(16 * i + 1, 16), 7 + 16 * j, :], 16, to_edges(0, 16))
+        choose(lambda i, j: field[pl.ds(16 * i + 1, 16), 24 + 16 * j, :], 16, to_edges(16, 16))
+
+    def prepare_faces(field):
         @pl.loop(0, 16)
         def _(u):
             def to_cubes(e, value):
                 cubes[e, pl.ds(pl.multiple_of(16 * u, 16), 16), :] = value
             choose(lambda i, j: field[16 * i + 1 + u, pl.ds(8 + 16 * j, 16), :], 16, to_cubes)
-            choose(lambda i, j: field[16 * i + 1 + u, pl.ds(7 + 16 * j, 1), :], 1, to_edges(u, 1))
-            choose(lambda i, j: field[16 * i + 1 + u, pl.ds(24 + 16 * j, 1), :], 1, to_edges(16 + u, 1))
+
+        @pl.loop(0, 4)
+        def _(entry):
+            high, low = split(cubes[entry])
+            zs = dot(jnp.concatenate([high, low], axis=1), picks[entry]).reshape(16, 16, 128)
+            blocks[entry, pl.ds(0, 16), :] = jnp.sum(jnp.where(y_row == y_lane, zs, 0.0), axis=1)
+
+    def make_picks():
+        @pl.loop(0, 4)
+        def _(entry):
+            z0 = inter[0, 3, entry]
+            pick = ((z_in == z0 - 1) & (z_out >= 32) & (z_out < 48)) | (
+                (z_in == z0 + 16) & (z_out >= 48) & (z_out < 64)
+            )
+            picks[entry] = jnp.where(pick, 1.0, 0.0).astype(bf16)
+            windows[entry] = jnp.where(z_in == z0 + lax.rem(z_out, 16), 1.0, 0.0).astype(bf16)
 
     def faces_of(ref, entry):
-        z0 = inter[0, 3, entry]
-        high, low = split(cubes[entry])
-        pick = ((z_in == z0 - 1) & (z_out >= 32) & (z_out < 48)) | (
-            (z_in == z0 + 16) & (z_out >= 48) & (z_out < 64)
-        )
-        pick = jnp.where(pick, 1.0, 0.0).astype(bf16)
-        zs = dot(jnp.concatenate([high, low], axis=1), pick).reshape(16, 16, 128)
-        zs = jnp.sum(jnp.where(y_row == y_lane, zs, 0.0), axis=1)
         high, low = split(edges[entry])
-        window = jnp.where(z_in == z0 + lax.rem(z_out, 16), 1.0, 0.0).astype(bf16)
-        flat = dot(jnp.concatenate([high, low], axis=1), window)
+        flat = dot(jnp.concatenate([high, low], axis=1), windows[entry])
+        zs = ref[pl.ds(0, 16), :]
         first = jnp.where(lane16 < 16, flat[0:16], jnp.where(lane16 < 32, flat[16:32], zs))
         x_lanes = (lane16 >= 64) & (lane16 < 80)
         ref[pl.ds(0, 16), :] = jnp.where(lane16 < 64, first, 0.0)
@@ -295,8 +311,6 @@
             old = before(x)
             new[x + 1, pl.ds(8, ny), :] = old + r2[x] * (c - old) + rc[x] * (nbs - 6.0 * c)
 
-    row = lax.broadcasted_iota(jnp.int32, (8, ROW), 0)
-
     def make_ghosts(f, phase, weight):
         parts = []
         for slot in range(2):
@@ -309,41 +323,54 @@
 
         @pl.loop(0, 9)
         def _(c):
-            cols = pl.ds(pl.multiple_of(c * 256, 256), 256)
-            ghost[:, cols] = dot(left, spread[:, cols])
-        for slot in range(2):
-            for k in range(2):
-                face = ghost[pl.ds(96 + 32 * slot + 16 * k, 16), :] * rows[...]
-                f[slot, pl.ds(7 + 49 * k, 1), pl.ds(EDGE, ROW)] = jnp.sum(face, axis=0, keepdims=True)
+            both = dot(left, spread[:, pl.ds(pl.multiple_of(c * 256, 256), 256)])
+            for half in range(2):
+                col = 2 * c + half
+                part = both[:, 128 * half:128 * half + 128]
+                ghost[col] = part[:96]
+                for slot in range(2):
+                    for k in range(2):
+                        first = 96 + 32 * slot + 16 * k
+                        face = part[first:first + 16] * rows[col]
+                        f[slot, col + 1, pl.ds(7 + 49 * k, 1), :] = jnp.sum(face, axis=0, keepdims=True)
+
+    lane8 = lax.broadcasted_iota(jnp.int32, (8, 128), 1)
+    under = {shift: lane8 < shift for shift in (1, 48, 80, 127)}
 
     def fine_update(f, g, slot):
         @pl.loop(0, 6)
         def _(i):
             base = pl.multiple_of(8 * i, 8)
-            prev = f[slot, pl.ds(base, 8), pl.ds(EDGE, ROW)]
-            after = f[slot, pl.ds(pl.multiple_of(base + 16, 8), 8), pl.ds(EDGE, ROW)]
-            wide = f[slot, pl.ds(pl.multiple_of(base + 8, 8), 8), :]
-            c = wide[:, EDGE:EDGE + ROW]
-            width = ROW + 2 * EDGE
-            nbs = jnp.where(row == 0, pltpu.roll(prev, 1, 0), pltpu.roll(c, 1, 0))
-            nbs = nbs + jnp.where(row == 7, pltpu.roll(after, 7, 0), pltpu.roll(c, 7, 0))
-            nbs = nbs + pltpu.roll(wide, FINE, 1)[:, EDGE:EDGE + ROW]
-            nbs = nbs + pltpu.roll(wide, width - FINE, 1)[:, EDGE:EDGE + ROW]
-            nbs = nbs + pltpu.roll(wide, 1, 1)[:, EDGE:EDGE + ROW] * inside[0]
-            nbs = nbs + pltpu.roll(wide, width - 1, 1)[:, EDGE:EDGE + ROW] * inside[1]
-            nbs = nbs + ghost[pl.ds(pl.multiple_of(48 * slot + base, 8), 8), :]
-            here = (slot, pl.ds(pl.multiple_of(base + 8, 8), 8), pl.ds(EDGE, ROW))
-            old = g[here]
-            rows_here = pl.ds(base, 8)
-            g[here] = old + fr2[slot, rows_here, :] * (c - old) + frc[slot, rows_here, :] * (nbs - 6.0 * c)
+
+            def turned(col):
+                value = f[slot, col, pl.ds(pl.multiple_of(base + 8, 8), 8), :]
+                return value, {shift: pltpu.roll(value, shift, 1) for shift in under}
+
+            _, before = turned(0)
+            c, here = turned(1)
+            for col in range(COLS):
+                later, after = turned(col + 2)
+                nbs = f[slot, col + 1, pl.ds(base + 7, 8), :] + f[slot, col + 1, pl.ds(base + 9, 8), :]
+                nbs = nbs + jnp.where(under[48], before[48], here[48])
+                nbs = nbs + jnp.where(under[80], here[80], after[80])
+                nbs = nbs + jnp.where(under[1], before[1], here[1]) * inside[col % 3, 0]
+                nbs = nbs + jnp.where(under[127], here[127], after[127]) * inside[col % 3, 1]
+                nbs = nbs + ghost[col, pl.ds(pl.multiple_of(48 * slot + base, 8), 8), :]
+                place = (slot, col + 1, pl.ds(pl.multiple_of(base + 8, 8), 8), slice(None))
+                old = g[place]
+                coef = (slot, col, pl.ds(base, 8), slice(None))
+                g[place] = old + fr2[coef] * (c - old) + frc[coef] * (nbs - 6.0 * c)
+                before, here, c = here, after, later
 
     def restrict(f, step):
-        lefts = []
-        for slot in range(2):
-            high, low = split(f[slot, pl.ds(8, FINE), pl.ds(EDGE, ROW)])
-            part = dot(down[...], jnp.concatenate([high, low], axis=0))
-            lefts.extend(split(part))
-        means = dot(jnp.concatenate(lefts, axis=0), gather[...])
+        means = jnp.zeros((64, 256), jnp.float32)
+        for pair in range(COLS // 2):
+            lefts = []
+            for slot in range(2):
+                cols = [f[slot, 2 * pair + 1 + k, pl.ds(8, FINE), :] for k in range(2)]
+                high, low = split(jnp.concatenate(cols, axis=1))
+                lefts.extend(split(dot(down[...], jnp.concatenate([high, low], axis=0))))
+            means = means + dot(jnp.concatenate(lefts, axis=0), gather[pl.ds(256 * pair, 256), :])
         for slot in range(2):
             mean = (means[32 * slot:32 * slot + 16] + means[32 * slot + 16:32 * slot + 32]) * (1.0 / 27.0)
             rest_out[step, slot] = mean
@@ -388,7 +415,9 @@
 
     loads[0].wait()
     send_halo(0, p0)
-    for load in loads[1:]:
+    make_picks()
+    prepare_faces(p0)
+    for load in loads[1:4]:
         load.wait()
 
     @pl.loop(0, nx)
@@ -397,13 +426,15 @@
         r2[x] = 2.0 * r
         rc[x] = rc[x] * r
 
+    for load in loads[4:]:
+        load.wait()
+
     for slot in range(2):
-        @pl.loop(0, 6)
-        def _(i):
-            at = (slot, pl.ds(pl.multiple_of(8 * i, 8), 8), slice(None))
-            r = 1.0 / (1.0 + fr2[at])
-            fr2[at] = 2.0 * r
-            frc[at] = frc[at] * r
+        @pl.loop(0, COLS)
+        def _(c):
+            r = 1.0 / (1.0 + fr2[slot, c])
+            fr2[slot, c] = 2.0 * r
+            frc[slot, c] = frc[slot, c] * r
 
     f, g = fa, fb
     stores = []
@@ -416,6 +447,7 @@
             def before(x):
                 return p0[x + 1, pl.ds(8, ny), :]
             send_halo(2, field)
+            prepare_faces(field)
         take_halo(2 * step, field)
         send_faces(2 * step, field)
         coarse_update(new, field, before)
@@ -423,6 +455,7 @@
         take_faces(2 * step)
         make_ghosts(f, step, 0.0)
         fine_update(f, g, 0)
+        prepare_faces(new)
         take_halo(2 * step + 1, new)
         send_faces(2 * step + 1, new)
         fine_update(f, g, 1)
@@ -435,13 +468,18 @@
             f, g = g, f
         restrict(f, step)
         if step == STEPS - 1:
-            stores.append(pltpu.make_async_copy(f.at[fmid], fnext_h, store_sem.at[0]))
-            stores.append(pltpu.make_async_copy(g.at[fmid], flast_h, store_sem.at[1]))
-            for store in stores[-2:]:
-                store.start()
+            for k, (src, dst) in enumerate([(f, fnext_h), (g, flast_h)]):
+                for c in range(COLS):
+                    store = pltpu.make_async_copy(
+                        src.at[:, c + 1, pl.ds(8, FINE), :],
+                        dst.at[:, :, pl.ds(128 * c, 128)],
+                        store_sem.at[2 + k * COLS + c],
+                    )
+                    store.start()
+                    stores.append(store)
         insert(new, step)
         out = next_h if step == STEPS - 1 else last_h
-        store = pltpu.make_async_copy(new.at[mid], out, store_sem.at[2 + step])
+        store = pltpu.make_async_copy(new.at[mid], out, store_sem.at[step])
         if step == STEPS - 1:
             store.start()
             stores.append(store)
@@ -462,6 +500,21 @@
     last_store.wait()
     for store in stores:
         store.wait()
+
+
+def hand_over(*refs):
+    sources, targets, sems = refs[:4], refs[4:8], refs[8]
+    copies = []
+    for src, dst in zip(sources, targets):
+        parts = 4 if src.shape[0] == 64 else 2
+        rows = src.shape[0] // parts
+        for k in range(parts):
+            at = pl.ds(k * rows, rows)
+            copies.append(pltpu.make_async_copy(src.at[at], dst.at[at], sems.at[len(copies)]))
+    for copy in copies:
+        copy.start()
+    for copy in copies:
+        copy.wait()
 
 
 def on_device(nt, nb, *args):
@@ -474,7 +527,7 @@
     hbm = pl.BlockSpec(memory_space=pl.ANY)
     shape_c, shape_f = coarse[0].shape, fine[0].shape
     dma = pltpu.SemaphoreType.DMA
-    return pl.pallas_call(
+    outs = pl.pallas_call(
         functools.partial(kernel, nt, nb),
         out_shape=[jax.ShapeDtypeStruct(s, f32) for s in (shape_c, shape_c, shape_f, shape_f)],
         in_specs=[smem, smem] + [hbm] * 8 + [vmem] * len(consts),
@@ -486,22 +539,24 @@
             pltpu.VMEM((64, 64, 128), f32),
             pltpu.VMEM((64, 64, 128), f32),
             pltpu.VMEM((64, 64, 128), f32),
-            pltpu.VMEM((2, 64, ROW + 2 * EDGE), f32),
-            pltpu.VMEM((2, 64, ROW + 2 * EDGE), f32),
-            pltpu.VMEM((2, FINE, ROW), f32),
-            pltpu.VMEM((2, FINE, ROW), f32),
+            pltpu.VMEM((2, COLS + 2, 64, 128), f32),
+            pltpu.VMEM((2, COLS + 2, 64, 128), f32),
+            pltpu.VMEM((2, COLS, FINE, 128), f32),
+            pltpu.VMEM((2, COLS, FINE, 128), f32),
             pltpu.VMEM((4, 4, 64, 128), f32),
             pltpu.VMEM((4, 4, 64, 128), f32),
             pltpu.VMEM((4, 3, 2, 48, 128), f32),
             pltpu.VMEM((4, 4, 2, 48, 128), f32),
             pltpu.VMEM((2, 2, 16, 256), f32),
             pltpu.VMEM((2, 4, 2, 16, 256), f32),
-            pltpu.VMEM((160, ROW), f32),
+            pltpu.VMEM((COLS, 96, 128), f32),
             pltpu.VMEM((4, 256, 128), f32),
             pltpu.VMEM((4, 256, 128), f32),
             pltpu.VMEM((4, 64, 128), f32),
+            pltpu.VMEM((4, 256, 128), bf16),
+            pltpu.VMEM((4, 256, 128), bf16),
             dma((4, 4)), dma((4, 4)), dma((4, 3)), dma((4, 3)), dma((2, 3)), dma((2, 3)),
-            dma((8,)), dma((4,)),
+            dma((4 + 4 * COLS,)), dma((2 + 2 * COLS,)),
         ],
         compiler_params=pltpu.CompilerParams(
             collective_id=0, has_side_effects=True, vmem_limit_bytes=56 * 1024 * 1024
@@ -509,6 +564,14 @@
         cost_estimate=pl.CostEstimate(flops=40_000_000, bytes_accessed=20_000_000, transcendentals=0),
         name="wave",
     )(inter, anchor, *coarse, *fine, *consts)
+    return pl.pallas_call(
+        hand_over,
+        out_shape=[jax.ShapeDtypeStruct(o.shape, f32) for o in outs],
+        in_specs=[hbm] * 4,
+        out_specs=[hbm] * 4,
+        scratch_shapes=[dma((12,))],
+        name="hand_over",
+    )(*outs)
 
 
 def solution(mesh):

time: 89.7 us -> 264 us (2.94)
  Pallas kernels: 81.9 us -> 263 us
  local copies, waits for them, and re-layouts: 6.92 us -> 0 us
    pallas_call x0 -> x1, Pallas kernels: none -> 182 us  [on_device(): pl.pallas_call(hand_over, out_shape=[jax.ShapeDtypeStruct(o.shape, f32) f...]
    unnamed x10 -> x0, local copies, waits for them, and re-layouts: 6.92 us -> none
where the time goes in v2:
time: 264 us
  Pallas kernels  263 us (100%)
    pallas_call x1, Pallas kernels, on_device(): pl.pallas_call(hand_over, out_shape=[jax.ShapeDtypeStruct(o.shape, f32) f...  182 us
    pallas_call x1, Pallas kernels, on_device(): pl.pallas_call(functools.partial(kernel, nt, nb), out_shape=[jax.ShapeDty...  81.1 us

profile of v2, /device:TPU:0, one launch (start us, length us, event | category | flops | bytes accessed | tf_op | source)
XLA Modules:
  0.0 263.6 jit_solution(5382977833234951083)
XLA Ops:
  0.6 81.1 %wave.1 = (f32[64,64,128]{2,1,0:T(8,128)}, f32[64,64,128]{2,1,0:T(8,128)}, f32[2,48,2304]{2,1,0:T(8,128)}, f32[2,48,2304]{2,1,0:T(8,128)}) custom-call(s32[1,4,4]{2,1,0:T(4,128)} %inter.1, s32[2,3]{1,0:T(2,128)} %anchor.1, f32[64,64,128]{2,1,0:T(8,128)} %now_h.1, f32[64,64,128]{2,1,0:T(8,128)} %before_h.1, f32[64,64,128]{2,1,0:T(8,128)} %courant_h.1, ...), custom_call_target="tpu_custom_call" | custom-call | flops 40000000 | bytes 20000000 | tf_op jit(solution)/shard_map/wave/pallas_call | solution.py:530
  81.7 181.9 %hand_over.1 = (f32[64,64,128]{2,1,0:T(8,128)}, f32[64,64,128]{2,1,0:T(8,128)}, f32[2,48,2304]{2,1,0:T(8,128)}, f32[2,48,2304]{2,1,0:T(8,128)}) custom-call(f32[64,64,128]{2,1,0:T(8,128)} %get-tuple-element.8.refs_0_, f32[64,64,128]{2,1,0:T(8,128)} %get-tuple-element.9.refs_1_, f32[2,48,2304]{2,1,0:T(8,128)} %get-tuple-element.10.refs_2_, ...), custom_call_target="tpu_custom_call" | custom-call | tf_op jit(solution)/shard_map/hand_over/pallas_call | solution.py:567

commit v3 on v2

--- a/solution.py
+++ b/solution.py
@@ -230,20 +230,20 @@
         choose(lambda i, j: field[pl.ds(16 * i + 1, 16), 24 + 16 * j, :], 16, to_edges(16, 16))
 
     def prepare_faces(field):
-        @pl.loop(0, 16)
+        @pl.loop(0, 16, unroll=2)
         def _(u):
             def to_cubes(e, value):
                 cubes[e, pl.ds(pl.multiple_of(16 * u, 16), 16), :] = value
             choose(lambda i, j: field[16 * i + 1 + u, pl.ds(8 + 16 * j, 16), :], 16, to_cubes)
 
-        @pl.loop(0, 4)
+        @pl.loop(0, 4, unroll=4)
         def _(entry):
             high, low = split(cubes[entry])
             zs = dot(jnp.concatenate([high, low], axis=1), picks[entry]).reshape(16, 16, 128)
             blocks[entry, pl.ds(0, 16), :] = jnp.sum(jnp.where(y_row == y_lane, zs, 0.0), axis=1)
 
     def make_picks():
-        @pl.loop(0, 4)
+        @pl.loop(0, 4, unroll=4)
         def _(entry):
             z0 = inter[0, 3, entry]
             pick = ((z_in == z0 - 1) & (z_out >= 32) & (z_out < 48)) | (
@@ -273,7 +273,7 @@
     def send_faces(phase, field):
         collect(field)
 
-        @pl.loop(0, 4)
+        @pl.loop(0, 4, unroll=4)
         def _(entry):
             faces_of(blocks.at[entry, pl.ds(0, 48), :], entry)
         for j in range(1, 4):
@@ -301,7 +301,7 @@
         return value
 
     def coarse_update(new, field, before):
-        @pl.loop(0, nx)
+        @pl.loop(0, nx, unroll=4)
         def _(x):
             c = field[x + 1, pl.ds(8, ny), :]
             nbs = field[x, pl.ds(8, ny), :] + field[x + 2, pl.ds(8, ny), :]
@@ -321,7 +321,7 @@
         high, low = split(jnp.concatenate(parts, axis=0))
         left = dot(up[...], jnp.concatenate([high, low], axis=1)).astype(bf16)
 
-        @pl.loop(0, 9)
+        @pl.loop(0, 9, unroll=9)
         def _(c):
             both = dot(left, spread[:, pl.ds(pl.multiple_of(c * 256, 256), 256)])
             for half in range(2):
@@ -338,7 +338,7 @@
     under = {shift: lane8 < shift for shift in (1, 48, 80, 127)}
 
     def fine_update(f, g, slot):
-        @pl.loop(0, 6)
+        @pl.loop(0, 6, unroll=2)
         def _(i):
             base = pl.multiple_of(8 * i, 8)
 
@@ -382,7 +382,7 @@
         for j in range(1, 4):
             rest_copy(step, j).wait_recv()
 
-        @pl.loop(0, 4)
+        @pl.loop(0, 4, unroll=4)
         def _(entry):
             value = rest_in[step, 0, 0]
             for j in range(4):
@@ -404,7 +404,7 @@
                     at = jnp.where(hit, lax.div(inter[0, 3, entry], 16), -1)
                     masks.append(place == at)
 
-                @pl.loop(0, 16)
+                @pl.loop(0, 16, unroll=16)
                 def _(x):
                     where = (16 * i + x + 1, pl.ds(8 + 16 * j, 16), slice(None))
                     value = new[where]
@@ -420,7 +420,7 @@
     for load in loads[1:4]:
         load.wait()
 
-    @pl.loop(0, nx)
+    @pl.loop(0, nx, unroll=8)
     def _(x):
         r = 1.0 / (1.0 + r2[x])
         r2[x] = 2.0 * r
@@ -430,7 +430,7 @@
         load.wait()
 
     for slot in range(2):
-        @pl.loop(0, COLS)
+        @pl.loop(0, COLS, unroll=6)
         def _(c):
             r = 1.0 / (1.0 + fr2[slot, c])
             fr2[slot, c] = 2.0 * r
@@ -503,18 +503,22 @@
 
 
 def hand_over(*refs):
-    sources, targets, sems = refs[:4], refs[4:8], refs[8]
-    copies = []
-    for src, dst in zip(sources, targets):
+    sources, targets, held, sems = refs[:4], refs[4:8], refs[8:12], refs[12]
+    loads, stores = [], []
+    for src, dst, mid in zip(sources, targets, held):
         parts = 4 if src.shape[0] == 64 else 2
         rows = src.shape[0] // parts
         for k in range(parts):
             at = pl.ds(k * rows, rows)
-            copies.append(pltpu.make_async_copy(src.at[at], dst.at[at], sems.at[len(copies)]))
-    for copy in copies:
-        copy.start()
-    for copy in copies:
-        copy.wait()
+            loads.append(pltpu.make_async_copy(src.at[at], mid.at[at], sems.at[0, len(loads)]))
+            stores.append(pltpu.make_async_copy(mid.at[at], dst.at[at], sems.at[1, len(stores)]))
+    for load in loads:
+        load.start()
+    for load, store in zip(loads, stores):
+        load.wait()
+        store.start()
+    for store in stores:
+        store.wait()
 
 
 def on_device(nt, nb, *args):
@@ -569,7 +573,8 @@
         out_shape=[jax.ShapeDtypeStruct(o.shape, f32) for o in outs],
         in_specs=[hbm] * 4,
         out_specs=[hbm] * 4,
-        scratch_shapes=[dma((12,))],
+        scratch_shapes=[pltpu.VMEM(o.shape, f32) for o in outs] + [dma((2, 12))],
+        compiler_params=pltpu.CompilerParams(vmem_limit_bytes=32 * 1024 * 1024),
         name="hand_over",
     )(*outs)
 

time: 264 us -> 72.4 us (0.27)
  Pallas kernels: 263 us -> 65.8 us
  local copies, waits for them, and re-layouts: 0 us -> 5.51 us
    pallas_call x1, Pallas kernels: 182 us -> 4.03 us  [on_device(): pl.pallas_call(hand_over, out_shape=[jax.ShapeDtypeStruct(o.shape, f32) f...]
    pallas_call x1, Pallas kernels: 81.1 us -> 61.8 us  [on_device(): pl.pallas_call(functools.partial(kernel, nt, nb), out_shape=[jax.ShapeDty...]
    unnamed x0 -> x8, local copies, waits for them, and re-layouts: none -> 5.51 us
where the time goes in v3:
time: 72.4 us; the launch traced here: 72.1 us
  Pallas kernels  65.8 us (91%)
  local copies, waits for them, and re-layouts  5.51 us (8%)
  between operations  0.81 us (1%)
    pallas_call x1, Pallas kernels, on_device(): pl.pallas_call(functools.partial(kernel, nt, nb), out_shape=[jax.ShapeDty...  61.8 us
    unnamed x8, local copies, waits for them, and re-layouts  5.51 us
    pallas_call x1, Pallas kernels, on_device(): pl.pallas_call(hand_over, out_shape=[jax.ShapeDtypeStruct(o.shape, f32) f...  4.03 us

profile of v3, /device:TPU:0, one launch (start us, length us, event | category | flops | bytes accessed | tf_op | source)
XLA Modules:
  0.0 72.1 jit_solution(17545858044698258378)
XLA Ops:
  0.6 61.8 %wave.1 = (f32[64,64,128]{2,1,0:T(8,128)}, f32[64,64,128]{2,1,0:T(8,128)}, f32[2,48,2304]{2,1,0:T(8,128)}, f32[2,48,2304]{2,1,0:T(8,128)}) custom-call(s32[1,4,4]{2,1,0:T(4,128)} %inter.1, s32[2,3]{1,0:T(2,128)} %anchor.1, f32[64,64,128]{2,1,0:T(8,128)} %now_h.1, f32[64,64,128]{2,1,0:T(8,128)} %before_h.1, f32[64,64,128]{2,1,0:T(8,128)} %courant_h.1, ...), custom_call_target="tpu_custom_call" | custom-call | flops 40000000 | bytes 20000000 | tf_op jit(solution)/shard_map/wave/pallas_call | solution.py:534
  62.4 0.0 copy-start
  62.4 1.6 %copy-done = f32[64,64,128]{2,1,0:T(8,128)S(1)} copy-done((f32[64,64,128]{2,1,0:T(8,128)S(1)}, f32[64,64,128]{2,1,0:T(8,128)}, u32[]{:S(2)}) %copy-start) | copy-done | bytes 2097176
  64.0 0.0 copy-start.1
  64.0 1.6 %copy-done.1 = f32[64,64,128]{2,1,0:T(8,128)S(1)} copy-done((f32[64,64,128]{2,1,0:T(8,128)S(1)}, f32[64,64,128]{2,1,0:T(8,128)}, u32[]{:S(2)}) %copy-start.1) | copy-done | bytes 2097176
  65.6 0.0 copy-start.2
  65.6 1.2 %copy-done.2 = f32[2,48,2304]{2,1,0:T(8,128)S(1)} copy-done((f32[2,48,2304]{2,1,0:T(8,128)S(1)}, f32[2,48,2304]{2,1,0:T(8,128)}, u32[]{:S(2)}) %copy-start.2) | copy-done | bytes 884760
  66.8 0.0 copy-start.3
  66.8 1.2 %copy-done.3 = f32[2,48,2304]{2,1,0:T(8,128)S(1)} copy-done((f32[2,48,2304]{2,1,0:T(8,128)S(1)}, f32[2,48,2304]{2,1,0:T(8,128)}, u32[]{:S(2)}) %copy-start.3) | copy-done | bytes 884760
  67.9 4.0 %hand_over.1 = (f32[64,64,128]{2,1,0:T(8,128)}, f32[64,64,128]{2,1,0:T(8,128)}, f32[2,48,2304]{2,1,0:T(8,128)}, f32[2,48,2304]{2,1,0:T(8,128)}) custom-call(f32[64,64,128]{2,1,0:T(8,128)S(1)} %copy-done, f32[64,64,128]{2,1,0:T(8,128)S(1)} %copy-done.1, f32[2,48,2304]{2,1,0:T(8,128)S(1)} %copy-done.2, f32[2,48,2304]{2,1,0:T(8,128)S(1)} %copy-done.3), custom_call_target="tpu_custom_call" | custom-call | tf_op jit(solution)/shard_map/hand_over/pallas_call | solution.py:571
Async XLA Ops:
  62.4 1.6 %copy-start = (f32[64,64,128]{2,1,0:T(8,128)S(1)}, f32[64,64,128]{2,1,0:T(8,128)}, u32[]{:S(2)}) copy-start(f32[64,64,128]{2,1,0:T(8,128)} %get-tuple-element.8.refs_0_) | copy-start | bytes 6291460
  64.0 1.6 %copy-start.1 = (f32[64,64,128]{2,1,0:T(8,128)S(1)}, f32[64,64,128]{2,1,0:T(8,128)}, u32[]{:S(2)}) copy-start(f32[64,64,128]{2,1,0:T(8,128)} %get-tuple-element.9.refs_1_) | copy-start | bytes 6291460
  65.6 1.2 %copy-start.2 = (f32[2,48,2304]{2,1,0:T(8,128)S(1)}, f32[2,48,2304]{2,1,0:T(8,128)}, u32[]{:S(2)}) copy-start(f32[2,48,2304]{2,1,0:T(8,128)} %get-tuple-element.10.refs_2_) | copy-start | bytes 2654212
  66.8 1.2 %copy-start.3 = (f32[2,48,2304]{2,1,0:T(8,128)S(1)}, f32[2,48,2304]{2,1,0:T(8,128)}, u32[]{:S(2)}) copy-start(f32[2,48,2304]{2,1,0:T(8,128)} %get-tuple-element.11.refs_3_) | copy-start | bytes 2654212

commit v4 on v3

--- a/solution.py
+++ b/solution.py
@@ -120,7 +120,6 @@
     peers = jnp.int32(2)
     for have in exists:
         peers = peers + jnp.where(have, 1, 0)
-    pl.semaphore_wait(barrier, peers)
 
     zero_side = jnp.zeros((2, 64, 128), jnp.float32)
     for buf in (fa, fb):
@@ -230,7 +229,7 @@
         choose(lambda i, j: field[pl.ds(16 * i + 1, 16), 24 + 16 * j, :], 16, to_edges(16, 16))
 
     def prepare_faces(field):
-        @pl.loop(0, 16, unroll=2)
+        @pl.loop(0, 16, unroll=4)
         def _(u):
             def to_cubes(e, value):
                 cubes[e, pl.ds(pl.multiple_of(16 * u, 16), 16), :] = value
@@ -301,7 +300,7 @@
         return value
 
     def coarse_update(new, field, before):
-        @pl.loop(0, nx, unroll=4)
+        @pl.loop(0, nx, unroll=8)
         def _(x):
             c = field[x + 1, pl.ds(8, ny), :]
             nbs = field[x, pl.ds(8, ny), :] + field[x + 2, pl.ds(8, ny), :]
@@ -338,7 +337,7 @@
     under = {shift: lane8 < shift for shift in (1, 48, 80, 127)}
 
     def fine_update(f, g, slot):
-        @pl.loop(0, 6, unroll=2)
+        @pl.loop(0, 6, unroll=3)
         def _(i):
             base = pl.multiple_of(8 * i, 8)
 
@@ -413,9 +412,10 @@
                         value = jnp.where(masks[entry], block, value)
                     new[where] = value
 
+    make_picks()
     loads[0].wait()
+    pl.semaphore_wait(barrier, peers)
     send_halo(0, p0)
-    make_picks()
     prepare_faces(p0)
     for load in loads[1:4]:
         load.wait()
@@ -574,7 +574,7 @@
         in_specs=[hbm] * 4,
         out_specs=[hbm] * 4,
         scratch_shapes=[pltpu.VMEM(o.shape, f32) for o in outs] + [dma((2, 12))],
-        compiler_params=pltpu.CompilerParams(vmem_limit_bytes=32 * 1024 * 1024),
+        compiler_params=pltpu.CompilerParams(vmem_limit_bytes=60 * 1024 * 1024),
         name="hand_over",
     )(*outs)
 

time: 72.4 us -> 67.6 us (0.934)
  local copies, waits for them, and re-layouts: 5.51 us -> 0 us
  Pallas kernels: 65.8 us -> 66.6 us
    unnamed x8 -> x0, local copies, waits for them, and re-layouts: 5.51 us -> none
    pallas_call x1, Pallas kernels: 4.03 us -> 5.31 us  [on_device(): pl.pallas_call(hand_over, out_shape=[jax.ShapeDtypeStruct(o.shape, f32) f...]
where the time goes in v4:
time: 67.6 us; the launch traced here: 67.4 us
  Pallas kernels  66.6 us (99%)
  between operations  0.8 us (1%)
    pallas_call x1, Pallas kernels, on_device(): pl.pallas_call(functools.partial(kernel, nt, nb), out_shape=[jax.ShapeDty...  61.3 us
    pallas_call x1, Pallas kernels, on_device(): pl.pallas_call(hand_over, out_shape=[jax.ShapeDtypeStruct(o.shape, f32) f...  5.31 us

profile of v4, /device:TPU:0, one launch (start us, length us, event | category | flops | bytes accessed | tf_op | source)
XLA Modules:
  0.0 67.4 jit_solution(12062907019653360860)
XLA Ops:
  0.6 61.3 %wave.1 = (f32[64,64,128]{2,1,0:T(8,128)}, f32[64,64,128]{2,1,0:T(8,128)}, f32[2,48,2304]{2,1,0:T(8,128)}, f32[2,48,2304]{2,1,0:T(8,128)}) custom-call(s32[1,4,4]{2,1,0:T(4,128)} %inter.1, s32[2,3]{1,0:T(2,128)} %anchor.1, f32[64,64,128]{2,1,0:T(8,128)} %now_h.1, f32[64,64,128]{2,1,0:T(8,128)} %before_h.1, f32[64,64,128]{2,1,0:T(8,128)} %courant_h.1, ...), custom_call_target="tpu_custom_call" | custom-call | flops 40000000 | bytes 20000000 | tf_op jit(solution)/shard_map/wave/pallas_call | solution.py:534
  62.0 5.3 %hand_over.1 = (f32[64,64,128]{2,1,0:T(8,128)}, f32[64,64,128]{2,1,0:T(8,128)}, f32[2,48,2304]{2,1,0:T(8,128)}, f32[2,48,2304]{2,1,0:T(8,128)}) custom-call(f32[64,64,128]{2,1,0:T(8,128)} %get-tuple-element.8.refs_0_, f32[64,64,128]{2,1,0:T(8,128)} %get-tuple-element.9.refs_1_, f32[2,48,2304]{2,1,0:T(8,128)} %get-tuple-element.10.refs_2_, ...), custom_call_target="tpu_custom_call" | custom-call | tf_op jit(solution)/shard_map/hand_over/pallas_call | solution.py:571
